TPU v7x, 32 devices: a whole 2x2x4 slice. The times are simulated.
32 devices in a mesh: row: 8 (over z, core), col: 4 (over y, x).
Axes of the slice: x: 2, y: 2, z: 4, core: 2. Of those that a mesh axis runs over, the one named last changes fastest.
Arguments:
- voxels: bfloat16 [8, 8, 16384], P('row', 'col'), may hold values from -6 to 6
- norm_gain: float32 [64], replicated, may hold values from 0.25 to 1.75
- in_weight: bfloat16 [64, 256], replicated, may hold values from -0.75 to 0.75
- conv_weight: float32 [6, 4, 128], replicated, may hold values from -3 to 3
- conv_bias: float32 [6, 128], replicated, may hold values from -3 to 3
- x_weight: bfloat16 [6, 128, 36], replicated, may hold values from -0.5 to 0.5
- dt_weight: float32 [6, 4, 128], replicated, may hold values from -3 to 3
- dt_bias: float32 [6, 128], replicated, may hold values from -6 to -1
- a_rate: float32 [6, 128, 16], replicated, may hold values from 0.1 to 4
- skip_gain: float32 [6, 128], replicated, may hold values from 0.5 to 1.5
- out_weight: bfloat16 [128, 64], replicated, may hold values from -0.5 to 0.5
Outputs:
- mixed: bfloat16 [8, 8, 16384], P('row', 'col')
All inputs are finite; a program needn't handle non-finite values.
Results may differ from a plain program's by a relative error of at most 0.013.
Values may be sent and summed in bfloat16 or wider, within the bound.
A program may use at most 64 MiB of HBM per device.

v0:
```python
import math

import jax
import jax.numpy as jnp
from jax import lax
from jax.sharding import PartitionSpec as P


def activation(line_rows, index, conv_weight, conv_bias):
    kernel = conv_weight.shape[1]
    length = line_rows.shape[1]
    values = line_rows.astype(jnp.float32)
    padded = jnp.pad(values, ((0, 0), (kernel - 1, 0), (0, 0)))
    preact = conv_bias[index]
    for offset in range(kernel):
        preact = preact + conv_weight[index, offset] * padded[:, offset : offset + length]
    return jax.nn.silu(preact).astype(jnp.bfloat16)


def run_direction(
    line_rows,
    index,
    reverse,
    conv_weight,
    conv_bias,
    x_weight,
    dt_weight,
    dt_bias,
    a_rate,
    skip_gain,
):
    ordered = line_rows[:, ::-1] if reverse else line_rows
    activated = activation(ordered, index, conv_weight, conv_bias)
    line_count, length, inner_width = activated.shape
    state_n = a_rate.shape[2]
    rank = dt_weight.shape[1]
    projected = jnp.dot(
        activated.reshape(-1, inner_width), x_weight[index], preferred_element_type=jnp.float32
    )
    projected = projected.reshape(line_count, length, -1)
    low_rank = projected[..., :rank]
    b_select = projected[..., rank : rank + state_n]
    c_select = projected[..., rank + state_n :]
    step_size = jax.nn.softplus(
        jnp.einsum("mlr,re->mle", low_rank, dt_weight[index], precision=lax.Precision.HIGHEST)
        + dt_bias[index]
    )
    decay_rate = a_rate[index]
    act_float = activated.astype(jnp.float32)
    block_len = math.gcd(length, 16)
    nblocks = length // block_len

    def regroup(array):
        return jnp.swapaxes(array.reshape(line_count, nblocks, block_len, array.shape[-1]), 0, 1)

    def advance(carried, inputs):
        step_block, act_block, b_block, c_block = inputs
        outputs = []
        for position in range(block_len):
            step_now = step_block[:, position]
            decays = jnp.exp(-step_now[:, :, None] * decay_rate)
            carried = (
                decays * carried
                + (step_now * act_block[:, position])[:, :, None] * b_block[:, position, None, :]
            )
            outputs.append(jnp.sum(carried * c_block[:, position, None, :], axis=2))
        return (carried, jnp.stack(outputs, axis=1))

    start = jnp.zeros((line_count, inner_width, state_n), jnp.float32)
    _, results = lax.scan(
        advance,
        start,
        (regroup(step_size), regroup(act_float), regroup(b_select), regroup(c_select)),
    )
    results = (
        jnp.swapaxes(results, 0, 1).reshape(line_count, length, inner_width)
        + skip_gain[index] * act_float
    )
    return results[:, ::-1] if reverse else results


def both_ways(line_rows, index, params):
    return run_direction(line_rows, index, False, *params) + run_direction(
        line_rows, index + 1, True, *params
    )


def project_inner(normed_rows, in_weight, inner_width):
    return jnp.dot(
        normed_rows, in_weight[:, :inner_width], preferred_element_type=jnp.float32
    ).astype(jnp.bfloat16)


def far_term(sum_rows, silu_gate, out_weight):
    far_hidden = (sum_rows.astype(jnp.float32) * silu_gate).astype(jnp.bfloat16)
    return jnp.dot(far_hidden, out_weight, preferred_element_type=jnp.float32).astype(jnp.bfloat16)


def local(
    voxels,
    norm_gain,
    in_weight,
    conv_weight,
    conv_bias,
    x_weight,
    dt_weight,
    dt_bias,
    a_rate,
    skip_gain,
    out_weight,
):
    params = (conv_weight, conv_bias, x_weight, dt_weight, dt_bias, a_rate, skip_gain)
    width = norm_gain.shape[0]
    inner_width = out_weight.shape[0]
    depth_loc, height_loc, merged = voxels.shape
    z_cells = merged // width
    values = voxels.reshape(depth_loc, height_loc, z_cells, width).astype(jnp.float32)
    normed = (
        values * lax.rsqrt(jnp.mean(values * values, axis=-1, keepdims=True) + 1e-05) * norm_gain
    ).astype(jnp.bfloat16)
    flat_rows = normed.reshape(-1, width)
    inner_z = project_inner(flat_rows, in_weight, inner_width).reshape(
        depth_loc, height_loc, z_cells, inner_width
    )
    gate = jnp.dot(flat_rows, in_weight[:, inner_width:], preferred_element_type=jnp.float32)
    silu_gate = jax.nn.silu(gate)
    along_z = both_ways(inner_z.reshape(depth_loc * height_loc, z_cells, inner_width), 0, params)
    inner_y = lax.all_to_all(inner_z, "col", split_axis=2, concat_axis=1, tiled=True)
    y_full = inner_y.shape[1]
    z_part = inner_y.shape[2]
    along_y = both_ways(
        inner_y.transpose(0, 2, 1, 3).reshape(depth_loc * z_part, y_full, inner_width), 2, params
    )
    sum_y = (
        along_y.reshape(depth_loc, z_part, y_full, inner_width)
        .transpose(0, 2, 1, 3)
        .astype(jnp.bfloat16)
    )
    inner_x, sum_y_x = (
        lax.all_to_all(inner_y, "row", split_axis=1, concat_axis=0, tiled=True),
        lax.all_to_all(sum_y, "row", split_axis=1, concat_axis=0, tiled=True),
    )
    x_full, y_part = (inner_x.shape[0], inner_x.shape[1])
    along_x = both_ways(
        inner_x.transpose(1, 2, 0, 3).reshape(y_part * z_part, x_full, inner_width), 4, params
    )
    along_x = along_x.reshape(y_part, z_part, x_full, inner_width).transpose(2, 0, 1, 3)
    sum_xy = (sum_y_x.astype(jnp.float32) + along_x).astype(jnp.bfloat16)
    returned = lax.all_to_all(
        lax.all_to_all(sum_xy, "row", split_axis=0, concat_axis=1, tiled=True),
        "col",
        split_axis=1,
        concat_axis=2,
        tiled=True,
    )
    far_part = far_term(returned.reshape(-1, inner_width), silu_gate, out_weight)
    near_hidden = (along_z.reshape(-1, inner_width) * silu_gate).astype(jnp.bfloat16)
    mixed = (
        jnp.dot(near_hidden, out_weight, preferred_element_type=jnp.float32)
        + far_part.astype(jnp.float32)
    ).astype(jnp.bfloat16)
    return mixed.reshape(depth_loc, height_loc, merged)


def solution(mesh):
    in_specs = (P("row", "col", None), P(), P(), P(), P(), P(), P(), P(), P(), P(), P())
    out_specs = P("row", "col", None)
    return jax.shard_map(local, mesh=mesh, in_specs=in_specs, out_specs=out_specs, check_vma=False)
```

profile of v0, /device:TPU:0, one launch (start us, length us, event | category | flops | bytes accessed | tf_op | source)
XLA Modules:
  0.0 114.8 jit_solution(4572390970896620632)
XLA Ops:
  3.2 5.3 %all-to-all-start = ((bf16[1,2,256,128]{3,1,0,2:T(2,128)(2,1)}), bf16[1,2,256,128]{3,1,0,2:T(2,128)(2,1)S(1)}, u32[]{:S(2)}, u32[]{:S(2)}) async-start(bf16[1,2,256,128]{3,1,0,2:T(2,128)(2,1)} %copy.89), calls=%async_computation | async-start | bytes 262144 | tf_op jit(solution)/shard_map/all_to_all | solution.py:128
  14.7 14.4 %while.7 = (s32[]{:T(128)}, f32[2,128,16]{1,2,0:T(8,128)S(1)}, f32[16,2,16,128]{3,2,0,1:T(8,128)S(1)}, f32[16,2,16,128]{3,1,2,0:T(2,128)S(1)}, f32[1,128,16]{1,2...) while((s32[]{:T(128)}, f32[2,128,16]{1,2,0:T(8,128)S(1)}, ...), condition=%wide.region_36.37_spmd.clone, body=%wide.region_19.36_spmd.clone.sunk | while | flops 602115 | bytes 493180 | solution.py:70
  31.0 14.4 %while.6 = (s32[]{:T(128)}, f32[2,128,16]{1,2,0:T(8,128)S(1)}, f32[16,2,16,128]{3,2,0,1:T(8,128)S(1)}, f32[16,2,16,128]{3,1,2,0:T(2,128)S(1)}, f32[1,128,16]{1,2...) while((s32[]{:T(128)}, f32[2,128,16]{1,2,0:T(8,128)S(1)}, ...), condition=%wide.region_18.19_spmd.clone, body=%wide.region_1.18_spmd.clone.sunk | while | flops 602115 | bytes 493180 | solution.py:70
  46.7 1.1 fusion.124
  49.1 1.1 fusion.125
  51.3 1.5 %multiply_reduce_fusion.52 = (f32[64,128]{1,0:T(8,128)S(1)}, f32[64,128]{1,0:T(8,128)S(1)}, f32[64,128]{1,0:T(8,128)S(1)}, f32[64,128]{1,0:T(8,128)S(1)}) fusion(f32[64,16]{1,0:T(8,128)S(1)} %bitcast.1051, f32[64,16]{1,0:T(8,128)S(1)} %bitcast.1009, f32[64,128]{1,0:T(8,128)S(1)} %bitcast.901, f32[64,128]{1,0:T(8,128)S(1)} %bitcast.1018, ...), kind=kLoop, calls=%fused_computation.302 | loop fusion | flops 3112960 | bytes 434176 | tf_op jit(solution)/shard_map/while/body/eval_jaxpr/reduce_sum | solution.py:66
  52.8 2.1 %multiply_reduce_fusion.48 = (f32[64,128]{1,0:T(8,128)S(1)}, f32[64,128]{1,0:T(8,128)S(1)}, f32[64,128]{1,0:T(8,128)S(1)}, f32[64,128]{1,0:T(8,128)S(1)}) fusion(f32[64,16]{1,0:T(8,128)S(1)} %bitcast.1002, f32[64,16]{1,0:T(8,128)S(1)} %bitcast.1003, f32[64,128]{1,0:T(8,128)S(1)} %bitcast.898, f32[64,128]{1,0:T(8,128)S(1)} %bitcast.1017, ...), kind=kLoop, calls=%fused_computation.295 | loop fusion | flops 5210112 | bytes 712704 | tf_op jit(solution)/shard_map/while/body/eval_jaxpr/reduce_sum | solution.py:66
  56.6 4.9 %all-to-all-start.2 = ((bf16[1,8,64,128]{3,2,0,1:T(8,128)(2,1)}), bf16[1,8,64,128]{3,2,0,1:T(8,128)(2,1)S(1)}, u32[]{:S(2)}, u32[]{:S(2)}) async-start(bf16[1,8,64,128]{3,2,0,1:T(8,128)(2,1)} %copy.95), calls=%async_computation.2 | async-start | bytes 262144 | tf_op jit(solution)/shard_map/all_to_all | solution.py:140
  61.5 1.4 %multiply_reduce_fusion.60 = (f32[64,128]{1,0:T(8,128)S(1)}, f32[64,128]{1,0:T(8,128)S(1)}, f32[64,128]{1,0:T(8,128)S(1)}, f32[64,128]{1,0:T(8,128)S(1)}) fusion(f32[64,16]{1,0:T(8,128)S(1)} %bitcast.981, f32[64,16]{1,0:T(8,128)S(1)} %bitcast.963, f32[64,128]{1,0:T(8,128)S(1)} %bitcast.879, f32[64,128]{1,0:T(8,128)S(1)} %bitcast.972, ...), kind=kLoop, calls=%fused_computation.317 | loop fusion | flops 3112960 | bytes 434176 | tf_op jit(solution)/shard_map/while/body/eval_jaxpr/reduce_sum | solution.py:66
  63.0 2.1 %multiply_reduce_fusion.56 = (f32[64,128]{1,0:T(8,128)S(1)}, f32[64,128]{1,0:T(8,128)S(1)}, f32[64,128]{1,0:T(8,128)S(1)}, f32[64,128]{1,0:T(8,128)S(1)}) fusion(f32[64,16]{1,0:T(8,128)S(1)} %bitcast.956, f32[64,16]{1,0:T(8,128)S(1)} %bitcast.957, f32[64,128]{1,0:T(8,128)S(1)} %bitcast.876, f32[64,128]{1,0:T(8,128)S(1)} %bitcast.971, ...), kind=kLoop, calls=%fused_computation.310 | loop fusion | flops 5210112 | bytes 712704 | tf_op jit(solution)/shard_map/while/body/eval_jaxpr/reduce_sum | solution.py:66
  66.8 1.5 %all-to-all-done.2 = bf16[1,8,64,128]{3,2,0,1:T(8,128)(2,1)S(1)} async-done(((bf16[1,8,64,128]{3,2,0,1:T(8,128)(2,1)}), bf16[1,8,64,128]{3,2,0,1:T(8,128)(2,1)S(1)}, u32[]{:S(2)}, u32[]{:S(2)}) %all-to-all-start.2) | async-done | bytes 131104 | tf_op jit(solution)/shard_map/all_to_all | solution.py:140
  68.3 3.6 %all-to-all-start.1 = ((bf16[1,8,64,128]{3,2,0,1:T(8,128)(2,1)}), bf16[1,8,64,128]{3,2,0,1:T(8,128)(2,1)S(1)}, u32[]{:S(2)}, u32[]{:S(2)}) async-start(bf16[1,8,64,128]{3,2,0,1:T(8,128)(2,1)} %copy.93), calls=%async_computation.1 | async-start | bytes 262144 | tf_op jit(solution)/shard_map/all_to_all | solution.py:141
  73.1 1.1 fusion.126
  74.9 1.1 compare_select_fusion.1
  77.8 1.1 fusion.127
  79.6 1.1 compare_select_fusion
  81.3 1.5 %multiply_reduce_fusion.36 = (f32[64,128]{1,0:T(8,128)S(1)}, f32[64,128]{1,0:T(8,128)S(1)}, f32[64,128]{1,0:T(8,128)S(1)}, f32[64,128]{1,0:T(8,128)S(1)}) fusion(f32[64,16]{1,0:T(8,128)S(1)} %bitcast.1047, f32[64,16]{1,0:T(8,128)S(1)} %bitcast.993, f32[64,128]{1,0:T(8,128)S(1)} %bitcast.916, f32[64,128]{1,0:T(8,128)S(1)} %bitcast.1027, ...), kind=kLoop, calls=%fused_computation.272 | loop fusion | flops 3112960 | bytes 434176 | tf_op jit(solution)/shard_map/while/body/eval_jaxpr/reduce_sum | solution.py:66
  82.8 2.1 %multiply_reduce_fusion.32 = (f32[64,128]{1,0:T(8,128)S(1)}, f32[64,128]{1,0:T(8,128)S(1)}, f32[64,128]{1,0:T(8,128)S(1)}, f32[64,128]{1,0:T(8,128)S(1)}) fusion(f32[64,16]{1,0:T(8,128)S(1)} %bitcast.986, f32[64,16]{1,0:T(8,128)S(1)} %bitcast.987, f32[64,128]{1,0:T(8,128)S(1)} %bitcast.913, f32[64,128]{1,0:T(8,128)S(1)} %bitcast.1026, ...), kind=kLoop, calls=%fused_computation.265 | loop fusion | flops 5210112 | bytes 712704 | tf_op jit(solution)/shard_map/while/body/eval_jaxpr/reduce_sum | solution.py:66
  86.0 2.1 %multiply_reduce_fusion.40 = (f32[64,128]{1,0:T(8,128)S(1)}, f32[64,128]{1,0:T(8,128)S(1)}, f32[64,128]{1,0:T(8,128)S(1)}, f32[64,128]{1,0:T(8,128)S(1)}) fusion(f32[64,16]{1,0:T(8,128)S(1)} %bitcast.948, f32[64,16]{1,0:T(8,128)S(1)} %bitcast.949, f32[64,128]{1,0:T(8,128)S(1)} %bitcast.891, f32[64,128]{1,0:T(8,128)S(1)} %bitcast.980, ...), kind=kLoop, calls=%fused_computation.280 | loop fusion | flops 5210112 | bytes 712704 | tf_op jit(solution)/shard_map/while/body/eval_jaxpr/reduce_sum | solution.py:66
  88.1 1.4 %multiply_reduce_fusion.44 = (f32[64,128]{1,0:T(8,128)S(1)}, f32[64,128]{1,0:T(8,128)S(1)}, f32[64,128]{1,0:T(8,128)S(1)}, f32[64,128]{1,0:T(8,128)S(1)}) fusion(f32[64,16]{1,0:T(8,128)S(1)} %bitcast.927, f32[64,16]{1,0:T(8,128)S(1)} %bitcast.929, f32[64,128]{1,0:T(8,128)S(1)} %bitcast.868, f32[64,128]{1,0:T(8,128)S(1)} %bitcast.940, ...), kind=kLoop, calls=%fused_computation.287 | loop fusion | flops 3112960 | bytes 434176 | tf_op jit(solution)/shard_map/while/body/eval_jaxpr/reduce_sum | solution.py:66
  91.4 5.1 %all-to-all-start.3 = ((bf16[8,1,64,128]{3,2,1,0:T(8,128)(2,1)}), bf16[8,1,64,128]{3,2,1,0:T(8,128)(2,1)}, u32[]{:S(2)}, u32[]{:S(2)}) async-start(bf16[8,1,64,128]{3,2,1,0:T(8,128)(2,1)} %copy.99), calls=%async_computation.3 | async-start | bytes 262144 | tf_op jit(solution)/shard_map/all_to_all | solution.py:150
  97.5 5.9 %all-to-all-done.3 = bf16[8,1,64,128]{3,2,1,0:T(8,128)(2,1)} async-done(((bf16[8,1,64,128]{3,2,1,0:T(8,128)(2,1)}), bf16[8,1,64,128]{3,2,1,0:T(8,128)(2,1)}, u32[]{:S(2)}, u32[]{:S(2)}) %all-to-all-start.3) | async-done | bytes 131104 | tf_op jit(solution)/shard_map/all_to_all | solution.py:150
  103.3 4.2 %all-to-all-start.4 = ((bf16[1,8,64,128]{3,2,0,1:T(8,128)(2,1)}), bf16[1,8,64,128]{3,2,0,1:T(8,128)(2,1)S(1)}, u32[]{:S(2)}, u32[]{:S(2)}) async-start(bf16[1,8,64,128]{3,2,0,1:T(8,128)(2,1)} %bitcast.272), calls=%async_computation.4 | async-start | bytes 262144 | tf_op jit(solution)/shard_map/all_to_all | solution.py:149
  108.4 4.2 %all-to-all-done.4 = bf16[1,8,64,128]{3,2,0,1:T(8,128)(2,1)S(1)} async-done(((bf16[1,8,64,128]{3,2,0,1:T(8,128)(2,1)}), bf16[1,8,64,128]{3,2,0,1:T(8,128)(2,1)S(1)}, u32[]{:S(2)}, u32[]{:S(2)}) %all-to-all-start.4) | async-done | bytes 131104 | tf_op jit(solution)/shard_map/all_to_all | solution.py:149
  (593 shorter events, 55.6 us)
Async XLA Ops:
  0.0 113.5 %copy-start = (bf16[128,64]{0,1:T(8,128)(2,1)S(1)}, bf16[128,64]{0,1:T(8,128)(2,1)}, u32[]{:S(2)}) copy-start(bf16[128,64]{0,1:T(8,128)(2,1)} %param.25) | copy-start | bytes 49156
  0.0 1.0 copy-start.1
  1.3 0.8 copy-start.5
  1.5 0.7 copy-start.25
  3.2 5.3 %copy-start.4 = (f32[6,4,128]{2,1,0:T(4,128)S(1)}, f32[6,4,128]{2,1,0:T(4,128)}, u32[]{:S(2)}) copy-start(f32[6,4,128]{2,1,0:T(4,128)} %param.18) | copy-start | bytes 36868
  3.2 42.8 %all-to-all-start = ((bf16[1,2,256,128]{3,1,0,2:T(2,128)(2,1)}), bf16[1,2,256,128]{3,1,0,2:T(2,128)(2,1)S(1)}, u32[]{:S(2)}, u32[]{:S(2)}) async-start(bf16[1,2,256,128]{3,1,0,2:T(2,128)(2,1)} %copy.89), calls=%async_computation | async-start | bytes 262144 | tf_op jit(solution)/shard_map/all_to_all | solution.py:128
  9.8 1.9 %copy-start.3 = (f32[6,128,16]{1,2,0:T(8,128)S(1)}, f32[6,128,16]{1,2,0:T(8,128)}, u32[]{:S(2)}) copy-start(f32[6,128,16]{1,2,0:T(8,128)} %param.23) | copy-start | bytes 147460
  9.8 0.7 copy-start.6
  9.8 1.2 %copy-start.7 = (f32[6,128]{1,0:T(8,128)S(1)}, f32[6,128]{1,0:T(8,128)}, u32[]{:S(2)}) copy-start(f32[6,128]{1,0:T(8,128)} %param.22) | copy-start | bytes 9220
  11.7 0.8 copy-start.2
  12.9 0.7 copy-start.29
  30.9 14.4 %copy-start.8 = (f32[6,128]{1,0:T(8,128)S(1)}, f32[6,128]{1,0:T(8,128)}, u32[]{:S(2)}) copy-start(f32[6,128]{1,0:T(8,128)} %param.24) | copy-start | bytes 9220
  56.6 11.7 %all-to-all-start.2 = ((bf16[1,8,64,128]{3,2,0,1:T(8,128)(2,1)}), bf16[1,8,64,128]{3,2,0,1:T(8,128)(2,1)S(1)}, u32[]{:S(2)}, u32[]{:S(2)}) async-start(bf16[1,8,64,128]{3,2,0,1:T(8,128)(2,1)} %copy.95), calls=%async_computation.2 | async-start | bytes 262144 | tf_op jit(solution)/shard_map/all_to_all | solution.py:140
  68.3 21.6 %all-to-all-start.1 = ((bf16[1,8,64,128]{3,2,0,1:T(8,128)(2,1)}), bf16[1,8,64,128]{3,2,0,1:T(8,128)(2,1)S(1)}, u32[]{:S(2)}, u32[]{:S(2)}) async-start(bf16[1,8,64,128]{3,2,0,1:T(8,128)(2,1)} %copy.93), calls=%async_computation.1 | async-start | bytes 262144 | tf_op jit(solution)/shard_map/all_to_all | solution.py:141
  72.0 0.7 copy-start.17
  72.0 0.7 copy-start.18
  72.0 0.7 copy-start.19
  74.2 0.7 copy-start.28
  76.7 0.7 copy-start.12
  78.9 0.7 copy-start.27
  89.9 0.7 copy-start.11
  91.4 12.0 %all-to-all-start.3 = ((bf16[8,1,64,128]{3,2,1,0:T(8,128)(2,1)}), bf16[8,1,64,128]{3,2,1,0:T(8,128)(2,1)}, u32[]{:S(2)}, u32[]{:S(2)}) async-start(bf16[8,1,64,128]{3,2,1,0:T(8,128)(2,1)} %copy.99), calls=%async_computation.3 | async-start | bytes 262144 | tf_op jit(solution)/shard_map/all_to_all | solution.py:150
  96.5 0.7 copy-start.10
  103.3 9.2 %all-to-all-start.4 = ((bf16[1,8,64,128]{3,2,0,1:T(8,128)(2,1)}), bf16[1,8,64,128]{3,2,0,1:T(8,128)(2,1)S(1)}, u32[]{:S(2)}, u32[]{:S(2)}) async-start(bf16[1,8,64,128]{3,2,0,1:T(8,128)(2,1)} %bitcast.272), calls=%async_computation.4 | async-start | bytes 262144 | tf_op jit(solution)/shard_map/all_to_all | solution.py:149
  (11 other events, 7.0 us)
where the time goes:
time: 116 us; the launch traced here: 115 us
  other arithmetic  41.9 us (36%)
  local copies, waits for them, and re-layouts  28.3 us (24%)
  starting transfers between devices  23 us (20%)
  waiting for transfers between devices  11.5 us (10%)
  matrix products  6.42 us (6%)
  loops' own time  2.86 us (2%)
    reduce_sum x168, other arithmetic, advance(): outputs.append(jnp.sum(carried * c_block[:, position, None, :], axis=2))  35.7 us
    unnamed x61, local copies, waits for them, and re-layouts  9.64 us
    all_to_all x1, waiting for transfers between devices, local(): lax.all_to_all(sum_xy, 'row', split_axis=0, concat_axis=1, tiled=True)  5.87 us
    all_to_all x1, starting transfers between devices, local(): lax.all_to_all(inner_z, 'col', split_axis=2, concat_axis=1, tiled=True)  5.29 us
    all_to_all x1, starting transfers between devices, local(): lax.all_to_all(sum_xy, 'row', split_axis=0, concat_axis=1, tiled=True)  5.08 us
    all_to_all x1, starting transfers between devices, local(): lax.all_to_all(inner_y, 'row', split_axis=1, concat_axis=0, tiled=True)  4.88 us
    slice x4, local copies, waits for them, and re-layouts, advance(): outputs.append(jnp.sum(carried * c_block[:, position, None, :], axis=2))  4.58 us
    dot_general x6, matrix products, run_direction(): jnp.einsum('mlr,re->mle', low_rank, dt_weight[index], precision=lax.Preci...  4.53 us
  transfers between devices with their start and end apart: 5, of which 3 were waited for; matrix products, arithmetic and copies ran while one was open for 45% of the time, Pallas kernels for 0%

commit v1 on v0

v1 whole, which is shorter than its diff:
```python
import functools

import jax
import jax.numpy as jnp
from jax import lax
from jax.experimental import pallas as pl
from jax.experimental.pallas import tpu as pltpu
from jax.sharding import PartitionSpec as P

MESH = pl.DeviceIdType.MESH
LOG2E = 1.4426950408889634
F32 = jnp.float32
BF16 = jnp.bfloat16


def silu(x):
    half = 0.5 * x
    return half + half * jnp.tanh(half)


def softplus(x):
    u = jnp.exp(-jnp.abs(x))
    return jnp.maximum(x, 0.0) + jnp.where(u < 1e-3, u - 0.5 * u * u, jnp.log(1.0 + u))


def column(tile, lane):
    return jnp.broadcast_to(tile[:, lane : lane + 1], tile.shape)


def kernel(
    sizes,
    vox_ref,
    gain_ref,
    inw_ref,
    convw_ref,
    convb_ref,
    xw_ref,
    dtw_ref,
    dtb_ref,
    rate_ref,
    skip_ref,
    outw_ref,
    out_ref,
    w4,
    ow2,
    xwp,
    dtwp,
    ratep,
    rates,
    nb,
    xs,
    yin,
    xin,
    yret,
    xret,
    yfar,
    xfar,
    inn,
    sgate,
    lstep,
    lu,
    lproj,
    lout,
    zinner,
    comb,
    zstep,
    zu,
    zproj,
    zskip,
    zout,
    zgate,
    acc,
    ysend,
    yrecv,
    xsend,
    xrecv,
    yrsend,
    yrrecv,
    xrsend,
    xrrecv,
):
    nrow, ncol, y_loc, half_z, zpy, zpx, width, inner, state, rank = sizes
    my_row, my_col = lax.axis_index("row"), lax.axis_index("col")
    z_cells = 2 * half_z

    barrier = pltpu.get_barrier_semaphore()
    for k in range(1, ncol):
        peer = lax.rem(my_col + k, ncol)
        pl.semaphore_signal(barrier, inc=1, device_id=(my_row, peer), device_id_type=MESH)
    for k in range(1, nrow):
        peer = lax.rem(my_row + k, nrow)
        pl.semaphore_signal(barrier, inc=1, device_id=(peer, my_col), device_id_type=MESH)

    values = vox_ref[...].astype(F32)
    squares = values * values
    lane = lax.broadcasted_iota(jnp.int32, values.shape, 1)
    low_half = lane < width
    mean_a = jnp.sum(jnp.where(low_half, squares, 0.0), axis=1, keepdims=True) * (1.0 / width)
    mean_b = jnp.sum(jnp.where(low_half, 0.0, squares), axis=1, keepdims=True) * (1.0 / width)
    scale = jnp.where(low_half, lax.rsqrt(mean_a + 1e-5), lax.rsqrt(mean_b + 1e-5))
    normed = values * scale * gain_ref[...]
    nb[...] = normed.astype(BF16).reshape(nb.shape)
    for r in range(nrow):
        pieces = [
            normed[y * half_z + r * zpx : y * half_z + (r + 1) * zpx] for y in range(y_loc)
        ]
        xs[r] = jnp.concatenate(pieces, axis=0).astype(BF16)

    pl.semaphore_wait(barrier, ncol - 1 + nrow - 1)

    def y_go(k):
        peer = lax.rem(my_col + k, ncol)
        return pltpu.make_async_remote_copy(
            src_ref=nb.at[:, pl.ds(pl.multiple_of(peer * zpy, zpy), zpy), :],
            dst_ref=yin.at[pl.ds(my_col * y_loc, y_loc)],
            send_sem=ysend.at[k],
            recv_sem=yrecv.at[k],
            device_id=(my_row, peer),
            device_id_type=MESH,
        )

    def x_go(k):
        peer = lax.rem(my_row + k, nrow)
        return pltpu.make_async_remote_copy(
            src_ref=xs.at[peer],
            dst_ref=xin.at[my_row],
            send_sem=xsend.at[k],
            recv_sem=xrecv.at[k],
            device_id=(peer, my_col),
            device_id_type=MESH,
        )

    def y_back(k):
        peer = lax.rem(my_col + k, ncol)
        return pltpu.make_async_remote_copy(
            src_ref=yret.at[pl.ds(peer * y_loc, y_loc)],
            dst_ref=yfar.at[my_col],
            send_sem=yrsend.at[k],
            recv_sem=yrrecv.at[k],
            device_id=(my_row, peer),
            device_id_type=MESH,
        )

    def x_back(k):
        peer = lax.rem(my_row + k, nrow)
        return pltpu.make_async_remote_copy(
            src_ref=xret.at[peer],
            dst_ref=xfar.at[my_row],
            send_sem=xrsend.at[k],
            recv_sem=xrrecv.at[k],
            device_id=(peer, my_col),
            device_id_type=MESH,
        )

    for k in range(1, ncol):
        y_go(k).start()
    for k in range(1, nrow):
        x_go(k).start()

    w4[...] = jnp.zeros_like(w4)
    w4[0:width, 0:inner] = inw_ref[:, 0:inner]
    w4[width : 2 * width, inner : 2 * inner] = inw_ref[:, 0:inner]
    w4[0:width, 2 * inner : 3 * inner] = inw_ref[:, inner : 2 * inner]
    w4[width : 2 * width, 3 * inner : 4 * inner] = inw_ref[:, inner : 2 * inner]
    ow2[...] = jnp.zeros_like(ow2)
    ow2[0:inner, 0:width] = outw_ref[...]
    ow2[inner : 2 * inner, width : 2 * width] = outw_ref[...]
    xwp[...] = jnp.zeros_like(xwp)
    xwp[:, :, 0 : rank + 2 * state] = xw_ref[...]
    dtwp[...] = jnp.zeros_like(dtwp)
    dtwp[:, 0:rank, :] = dtw_ref[...]
    for d in range(6):
        ratep[...] = jnp.zeros_like(ratep)
        ratep[:, 0:state] = rate_ref[d] * (-LOG2E)
        rates[d] = ratep[...].T[0:state]

    rows = 2 * 2 * y_loc
    front = rows // 2
    row8 = lax.broadcasted_iota(jnp.int32, (rows, inner), 0)
    forward8 = row8 < front
    lowhalf8 = lax.rem(row8, 2) == 0

    full = jnp.dot(nb[...].reshape(y_loc * half_z, 2 * width), w4[...], preferred_element_type=F32)
    zgate[...] = silu(full[:, 2 * inner :])
    for par in range(2):
        own = full[:, par * inner : (par + 1) * inner].astype(BF16).astype(F32)
        for y in range(y_loc):
            piece = own[y * half_z : (y + 1) * half_z]
            for direction in range(2):
                for low in range(2):
                    start = par * rows + direction * front + y * 2 + low
                    zinner[pl.ds(start, half_z, stride=2 * rows), :] = piece
    taps = convw_ref.shape[1]
    pad = taps - 1
    comb[0 : pad * rows, :] = jnp.zeros((pad * rows, inner), F32)

    @pl.loop(0, z_cells // 8)
    def _(block):
        for i in range(8):
            t = block * 8 + i
            up = zinner[pl.ds(pl.multiple_of(t * rows, rows), rows), :]
            down = zinner[pl.ds(pl.multiple_of((z_cells - 1 - t) * rows, rows), rows), :]
            comb[pl.ds(pl.multiple_of((t + pad) * rows, rows), rows), :] = jnp.where(
                forward8, up, down
            )

    def by_dir(a, b):
        return jnp.where(forward8, a, b)

    zconv = [by_dir(convw_ref[0, k : k + 1, :], convw_ref[1, k : k + 1, :]) for k in range(taps)]
    zbias = by_dir(convb_ref[0:1, :], convb_ref[1:2, :])
    zdtb = by_dir(dtb_ref[0:1, :], dtb_ref[1:2, :])
    zskipw = jnp.where(lowhalf8, by_dir(skip_ref[0:1, :], skip_ref[1:2, :]), 0.0)
    chunk = 32

    @pl.loop(0, z_cells // chunk)
    def _(block):
        base = pl.multiple_of(block * (chunk * rows), chunk * rows)
        pre = zbias[None]
        for k in range(taps):
            tap = comb[pl.ds(base + k * rows, chunk * rows), :]
            pre = pre + zconv[k][None] * tap.reshape(chunk, rows, inner)
        act_b = silu(pre).reshape(chunk * rows, inner).astype(BF16)
        act = act_b.astype(F32)
        row = lax.broadcasted_iota(jnp.int32, (chunk * rows, inner), 0)
        forward = lax.rem(row, rows) < front
        low = lax.rem(row, 2) == 0
        p0 = jnp.dot(act_b, xwp[0], preferred_element_type=F32)
        p1 = jnp.dot(act_b, xwp[1], preferred_element_type=F32)
        proj = jnp.where(forward, p0, p1)
        s0 = jnp.dot(proj, dtwp[0], precision=lax.Precision.HIGHEST, preferred_element_type=F32)
        s1 = jnp.dot(proj, dtwp[1], precision=lax.Precision.HIGHEST, preferred_element_type=F32)
        step = jnp.where(forward, s0, s1).reshape(chunk, rows, inner) + zdtb[None]
        step = softplus(step).reshape(chunk * rows, inner)
        here = pl.ds(base, chunk * rows)
        zstep[here, :] = step
        zu[here, :] = step * act
        zproj[here, :] = jnp.where(low, proj, pltpu.roll(proj, inner - state // 2, axis=1))
        zskip[here, :] = (act.reshape(chunk, rows, inner) * zskipw[None]).reshape(
            chunk * rows, inner
        )

    def lines(src_ref, ret_ref, d):
        length, pairs = src_ref.shape[0], src_ref.shape[1]
        count = 2 * pairs
        total = length * count
        both = jnp.dot(
            src_ref[...].reshape(length * pairs, 2 * width), w4[...], preferred_element_type=F32
        )
        inn[0:pad] = jnp.zeros((pad, count, inner), F32)
        inn[pad + length :] = jnp.zeros((pad, count, inner), F32)
        for par in range(2):
            part = both[:, par * inner : (par + 1) * inner].astype(BF16).astype(F32)
            inn[pad : pad + length, par * pairs : (par + 1) * pairs, :] = part.reshape(
                length, pairs, inner
            )
            gate = both[:, (2 + par) * inner : (3 + par) * inner]
            sgate[:, par * pairs : (par + 1) * pairs, :] = silu(gate).reshape(length, pairs, inner)
        for direction in range(2):
            e = d + direction
            pre = convb_ref[e : e + 1, :][None]
            for k in range(taps):
                first = k if direction == 0 else 2 * pad - k
                pre = pre + convw_ref[e, k : k + 1, :][None] * inn[first : first + length]
            act_b = silu(pre).reshape(total, inner).astype(BF16)
            act = act_b.astype(F32)
            proj = jnp.dot(act_b, xwp[e], preferred_element_type=F32)
            low = jnp.dot(
                proj, dtwp[e], precision=lax.Precision.HIGHEST, preferred_element_type=F32
            )
            step = softplus(low + dtb_ref[e : e + 1, :])
            lstep[...] = step.reshape(lstep.shape)
            lu[...] = (step * act).reshape(lu.shape)
            lproj[...] = proj.reshape(lproj.shape)
            skipped = (act * skip_ref[e : e + 1, :]).reshape(lout.shape)
            if direction == 0:
                lout[...] = skipped
            else:
                lout[...] += skipped

            @pl.loop(0, count // 8)
            def _(group):
                at = pl.ds(pl.multiple_of(group * 8, 8), 8)
                held = [jnp.zeros((8, inner), F32) for _ in range(state)]
                for i in range(length):
                    t = i if direction == 0 else length - 1 - i
                    step_t, u_t, proj_t = lstep[t, at, :], lu[t, at, :], lproj[t, at, :]
                    result = lout[t, at, :]
                    for n in range(state):
                        inflow = u_t * column(proj_t, rank + n)
                        if i == 0:
                            held[n] = inflow
                        else:
                            decay = jnp.exp2(step_t * rates[e, n : n + 1, :])
                            held[n] = decay * held[n] + inflow
                        result = result + held[n] * column(proj_t, rank + state + n)
                    lout[t, at, :] = result

        hidden = [
            (lout[:, par * pairs : (par + 1) * pairs, :] * sgate[:, par * pairs : (par + 1) * pairs, :])
            .reshape(length * pairs, inner)
            .astype(BF16)
            for par in range(2)
        ]
        far = jnp.dot(jnp.concatenate(hidden, axis=1), ow2[...], preferred_element_type=F32)
        ret_ref[...] = far.astype(BF16).reshape(ret_ref.shape)

    for y in range(y_loc):
        yin[my_col * y_loc + y] = nb[y, pl.ds(pl.multiple_of(my_col * zpy, zpy), zpy), :]
    for k in range(1, ncol):
        y_go(k).wait()
    lines(yin, yret, 2)
    for k in range(1, ncol):
        y_back(k).start()
    xin[my_row] = xs[my_row]
    for k in range(1, nrow):
        x_go(k).wait()
    lines(xin, xret, 4)
    for k in range(1, nrow):
        x_back(k).start()

    halves = state // 2
    zrate = [
        jnp.where(
            lowhalf8,
            by_dir(rates[0, n : n + 1, :], rates[1, n : n + 1, :]),
            by_dir(rates[0, halves + n : halves + n + 1, :], rates[1, halves + n : halves + n + 1, :]),
        )
        for n in range(halves)
    ]
    unroll = 8

    def advance(block, held):
        held = list(held)
        for i in range(unroll):
            t = block * unroll + i
            at = pl.ds(pl.multiple_of(t * rows, rows), rows)
            step_t, u_t, proj_t = zstep[at, :], zu[at, :], zproj[at, :]
            result = zskip[at, :]
            for n in range(halves):
                decay = jnp.exp2(step_t * zrate[n])
                held[n] = decay * held[n] + u_t * column(proj_t, rank + n)
                result = result + held[n] * column(proj_t, rank + state + n)
            zout[pl.ds(pl.multiple_of(t * rows, rows), front), :] = result[0:front]
            zout[pl.ds((z_cells - 1 - t) * rows + front, front), :] = result[front:]
        return tuple(held)

    lax.fori_loop(
        0,
        z_cells // unroll,
        advance,
        tuple(jnp.zeros((rows, inner), F32) for _ in range(halves)),
    )

    near = []
    for par in range(2):
        pieces = []
        for y in range(y_loc):
            total = None
            for direction in range(2):
                for low in range(2):
                    start = par * rows + direction * front + y * 2 + low
                    part = zout[pl.ds(start, half_z, stride=2 * rows), :]
                    total = part if total is None else total + part
            pieces.append(total)
        along = jnp.concatenate(pieces, axis=0)
        near.append((along * zgate[:, par * inner : (par + 1) * inner]).astype(BF16))
    acc[...] = jnp.dot(jnp.concatenate(near, axis=1), ow2[...], preferred_element_type=F32)

    yfar[my_col] = yret[pl.ds(my_col * y_loc, y_loc)]
    xfar[my_row] = xret[my_row]
    for k in range(1, ncol):
        y_back(k).wait()
    for c in range(ncol):
        for y in range(y_loc):
            acc[y * half_z + c * zpy : y * half_z + (c + 1) * zpy, :] += yfar[c, y].astype(F32)
    for k in range(1, nrow):
        x_back(k).wait()
    for r in range(nrow):
        part = xfar[r].astype(F32)
        for y in range(y_loc):
            acc[y * half_z + r * zpx : y * half_z + (r + 1) * zpx, :] += part[
                y * zpx : (y + 1) * zpx
            ]
    out_ref[...] = acc[...].astype(BF16)


def solution(mesh):
    nrow, ncol = mesh.shape["row"], mesh.shape["col"]

    def local(
        voxels,
        norm_gain,
        in_weight,
        conv_weight,
        conv_bias,
        x_weight,
        dt_weight,
        dt_bias,
        a_rate,
        skip_gain,
        out_weight,
    ):
        width = norm_gain.shape[0]
        inner = out_weight.shape[0]
        state, rank = a_rate.shape[2], dt_weight.shape[1]
        x_loc, y_loc, merged = voxels.shape
        assert x_loc == 1 and y_loc == 2
        z_cells = merged // width
        half_z = z_cells // 2
        zpy, zpx = half_z // ncol, half_z // nrow
        y_full = ncol * y_loc
        assert y_full == nrow and zpy == y_loc * zpx
        tokens = y_loc * half_z
        sizes = (nrow, ncol, y_loc, half_z, zpy, zpx, width, inner, state, rank)
        pairs = voxels.reshape(tokens, 2 * width)
        gain = jnp.concatenate([norm_gain, norm_gain]).reshape(1, 2 * width)
        line = (nrow, 2 * zpy, inner)
        zrows = 4 * y_loc * z_cells
        taps = conv_weight.shape[1]
        vmem = pl.BlockSpec(memory_space=pltpu.VMEM)
        out = pl.pallas_call(
            functools.partial(kernel, sizes),
            out_shape=jax.ShapeDtypeStruct((tokens, 2 * width), BF16),
            in_specs=[vmem] * 11,
            out_specs=vmem,
            scratch_shapes=[
                pltpu.VMEM((2 * width, 4 * inner), BF16),
                pltpu.VMEM((2 * inner, 2 * width), BF16),
                pltpu.VMEM((6, inner, 128), BF16),
                pltpu.VMEM((6, 128, inner), F32),
                pltpu.VMEM((inner, 128), F32),
                pltpu.VMEM((6, state, inner), F32),
                pltpu.VMEM((y_loc, half_z, 2 * width), BF16),
                pltpu.VMEM((nrow, y_loc * zpx, 2 * width), BF16),
                pltpu.VMEM((y_full, zpy, 2 * width), BF16),
                pltpu.VMEM((nrow, y_loc * zpx, 2 * width), BF16),
                pltpu.VMEM((y_full, zpy, 2 * width), BF16),
                pltpu.VMEM((nrow, y_loc * zpx, 2 * width), BF16),
                pltpu.VMEM((ncol, y_loc, zpy, 2 * width), BF16),
                pltpu.VMEM((nrow, y_loc * zpx, 2 * width), BF16),
                pltpu.VMEM((nrow + 2 * (taps - 1), 2 * zpy, inner), F32),
                pltpu.VMEM(line, F32),
                pltpu.VMEM(line, F32),
                pltpu.VMEM(line, F32),
                pltpu.VMEM(line, F32),
                pltpu.VMEM(line, F32),
                pltpu.VMEM((zrows, inner), F32),
                pltpu.VMEM((zrows + (taps - 1) * 4 * y_loc, inner), F32),
                pltpu.VMEM((zrows, inner), F32),
                pltpu.VMEM((zrows, inner), F32),
                pltpu.VMEM((zrows, inner), F32),
                pltpu.VMEM((zrows, inner), F32),
                pltpu.VMEM((zrows, inner), F32),
                pltpu.VMEM((tokens, 2 * inner), F32),
                pltpu.VMEM((tokens, 2 * width), F32),
                pltpu.SemaphoreType.DMA((ncol,)),
                pltpu.SemaphoreType.DMA((ncol,)),
                pltpu.SemaphoreType.DMA((nrow,)),
                pltpu.SemaphoreType.DMA((nrow,)),
                pltpu.SemaphoreType.DMA((ncol,)),
                pltpu.SemaphoreType.DMA((ncol,)),
                pltpu.SemaphoreType.DMA((nrow,)),
                pltpu.SemaphoreType.DMA((nrow,)),
            ],
            compiler_params=pltpu.CompilerParams(
                collective_id=0, has_side_effects=True, vmem_limit_bytes=40 * 1024 * 1024
            ),
        )(
            pairs,
            gain,
            in_weight,
            conv_weight,
            conv_bias,
            x_weight,
            dt_weight,
            dt_bias,
            a_rate,
            skip_gain,
            out_weight,
        )
        return out.reshape(voxels.shape)

    in_specs = (P("row", "col", None), P(), P(), P(), P(), P(), P(), P(), P(), P(), P())
    return jax.shard_map(
        local, mesh=mesh, in_specs=in_specs, out_specs=P("row", "col", None), check_vma=False
    )
```

time: 116 us -> 46.5 us (0.40)
  Pallas kernels: 0 us -> 41.4 us
  other arithmetic: 41.9 us -> 0.8 us
  local copies, waits for them, and re-layouts: 28.3 us -> 3.91 us
  starting transfers between devices: 23 us -> 0 us
  waiting for transfers between devices: 11.5 us -> 0 us
  matrix products: 6.42 us -> 0 us
  loops' own time: 2.86 us -> 0 us
    pallas_call x0 -> x1, Pallas kernels: none -> 41.4 us  [local(): pl.pallas_call(functools.partial(kernel, sizes), out_shape=jax.ShapeDtype...]
    reduce_sum x169 -> x0, other arithmetic: 35.9 us -> none  [the longest x168 35.7 us: advance(): outputs.append(jnp.sum(carried * c_block[:, position, None, :], axis=2))]
    all_to_all x5 -> x0, starting transfers between devices: 23 us -> none  [the longest x1 5.29 us: local(): lax.all_to_all(inner_z, 'col', split_axis=2, concat_axis=1, tiled=True)]
    all_to_all x5 -> x0, waiting for transfers between devices: 11.5 us -> none  [the longest x1 5.87 us: local(): lax.all_to_all(sum_xy, 'row', split_axis=0, concat_axis=1, tiled=True)]
    unnamed x61 -> x19, local copies, waits for them, and re-layouts: 9.64 us -> 2.36 us
    dot_general x16 -> x0, matrix products: 6.42 us -> none  [the longest x6 4.53 us: run_direction(): jnp.einsum('mlr,re->mle', low_rank, dt_weight[index], precision=lax.Preci...]
    slice x7 -> x0, local copies, waits for them, and re-layouts: 4.62 us -> none  [the longest x4 4.58 us: advance(): outputs.append(jnp.sum(carried * c_block[:, position, None, :], axis=2))]
    another operation x38 -> x0, local copies, waits for them, and re-layouts: 3.49 us -> none  [the longest x36 3.45 us: advance(): return (carried, jnp.stack(outputs, axis=1))]
  transfers between devices with their start and end apart: 5 -> 0, of which waited for: 3 -> 0; matrix products, arithmetic and copies ran while one was open for 45% -> 0% of each run, Pallas kernels for 0% -> 0%
where the time goes in v1:
time: 46.5 us; the launch traced here: 46.2 us
  Pallas kernels  41.4 us (89%)
  local copies, waits for them, and re-layouts  3.91 us (8%)
  other arithmetic  0.8 us (2%)
    pallas_call x1, Pallas kernels, local(): pl.pallas_call(functools.partial(kernel, sizes), out_shape=jax.ShapeDtype...  41.4 us
    unnamed x19, local copies, waits for them, and re-layouts  2.36 us

profile of v1, /device:TPU:0, one launch (start us, length us, event | category | flops | bytes accessed | tf_op | source)
XLA Modules:
  0.0 46.2 jit_solution(14070586362761582103)
XLA Ops:
  0.0 0.8 %maximum_bitcast_fusion.gain_ref = f32[1,128]{1,0:T(1,128)S(1)} fusion(f32[64]{0:T(128)} %param.12), kind=kLoop, calls=%fused_computation | loop fusion | flops 128 | bytes 768 | tf_op jit(solution)/shard_map/reshape | solution.py:417
  0.8 0.8 %copy.14.outw_ref = bf16[128,64]{1,0:T(8,128)(2,1)S(1)} copy(bf16[128,64]{0,1:T(8,128)(2,1)} %param.21) | data formatting | bytes 32768 | tf_op args[10]
  1.6 0.0 copy-start.6
  1.6 0.9 %reshape.9.vox_ref = bf16[256,128]{1,0:T(8,128)(2,1)S(1)} reshape(bf16[1,2,16384]{2,1,0:T(2,128)(2,1)} %param.11) | data formatting | bytes 131072 | tf_op jit(solution)/shard_map/reshape | solution.py:416
  2.5 0.0 copy-done.6
  2.6 0.0 copy-start.7
  2.6 0.2 copy.12.xw_ref
  2.8 0.6 %copy-done.7 = f32[6,128,16]{1,2,0:T(8,128)S(1)} copy-done((f32[6,128,16]{1,2,0:T(8,128)S(1)}, f32[6,128,16]{1,2,0:T(8,128)}, u32[]{:S(2)}) %copy-start.7) | copy-done | bytes 49176
  3.4 0.0 copy-start
  3.4 0.0 copy-start.1
  3.4 0.0 copy-start.2
  3.4 0.0 copy-start.3
  3.4 0.0 copy-start.4
  3.4 0.0 copy-start.5
  3.4 0.2 copy.13.rate_ref
  3.6 0.6 %copy-done = bf16[64,256]{1,0:T(8,128)(2,1)S(1)} copy-done((bf16[64,256]{1,0:T(8,128)(2,1)S(1)}, bf16[64,256]{1,0:T(8,128)(2,1)}, u32[]{:S(2)}) %copy-start) | copy-done | bytes 32792
  4.1 0.0 copy-done.1
  4.1 0.0 copy-done.2
  4.1 0.0 copy-done.3
  4.1 0.0 copy-done.4
  4.1 0.0 copy-done.5
  4.1 41.4 %shard_map.109 = bf16[256,128]{1,0:T(8,128)(2,1)S(1)} custom-call(bf16[256,128]{1,0:T(8,128)(2,1)S(1)} %reshape.9.vox_ref, f32[1,128]{1,0:T(1,128)S(1)} %maximum_bitcast_fusion.gain_ref, bf16[64,256]{1,0:T(8,128)(2,1)S(1)} %copy-done, f32[6,4,128]{2,1,0:T(4,128)S(1)} %copy-done.1, f32[6,128]{1,0:T(8,128)S(1)} %copy-done.3, ...), custom_call_target="tpu_custom_call" | custom-call | tf_op jit(solution)/shard_map/pallas_call | solution.py:422
  45.5 0.7 %reshape.11 = bf16[1,2,16384]{2,1,0:T(2,128)(2,1)} reshape(bf16[256,128]{1,0:T(8,128)(2,1)S(1)} %shard_map.109) | data formatting | bytes 131072 | tf_op jit(solution)/shard_map/reshape | solution.py:482
Async XLA Ops:
  1.6 0.9 %copy-start.6 = (bf16[6,128,36]{1,2,0:T(8,128)(2,1)S(1)}, bf16[6,128,36]{1,2,0:T(8,128)(2,1)}, u32[]{:S(2)}) copy-start(bf16[6,128,36]{1,2,0:T(8,128)(2,1)} %param.16) | copy-start | bytes 165892
  2.6 0.8 %copy-start.7 = (f32[6,128,16]{1,2,0:T(8,128)S(1)}, f32[6,128,16]{1,2,0:T(8,128)}, u32[]{:S(2)}) copy-start(f32[6,128,16]{1,2,0:T(8,128)} %param.19) | copy-start | bytes 147460
  3.4 0.8 %copy-start = (bf16[64,256]{1,0:T(8,128)(2,1)S(1)}, bf16[64,256]{1,0:T(8,128)(2,1)}, u32[]{:S(2)}) copy-start(bf16[64,256]{1,0:T(8,128)(2,1)} %inw_ref.1) | copy-start | bytes 98308
  3.4 0.8 %copy-start.1 = (f32[6,4,128]{2,1,0:T(4,128)S(1)}, f32[6,4,128]{2,1,0:T(4,128)}, u32[]{:S(2)}) copy-start(f32[6,4,128]{2,1,0:T(4,128)} %convw_ref.1) | copy-start | bytes 36868
  3.4 0.8 %copy-start.2 = (f32[6,4,128]{2,1,0:T(4,128)S(1)}, f32[6,4,128]{2,1,0:T(4,128)}, u32[]{:S(2)}) copy-start(f32[6,4,128]{2,1,0:T(4,128)} %dtw_ref.1) | copy-start | bytes 36868
  3.4 0.8 %copy-start.3 = (f32[6,128]{1,0:T(8,128)S(1)}, f32[6,128]{1,0:T(8,128)}, u32[]{:S(2)}) copy-start(f32[6,128]{1,0:T(8,128)} %convb_ref.1) | copy-start | bytes 9220
  3.4 0.8 %copy-start.4 = (f32[6,128]{1,0:T(8,128)S(1)}, f32[6,128]{1,0:T(8,128)}, u32[]{:S(2)}) copy-start(f32[6,128]{1,0:T(8,128)} %dtb_ref.1) | copy-start | bytes 9220
  3.4 0.8 %copy-start.5 = (f32[6,128]{1,0:T(8,128)S(1)}, f32[6,128]{1,0:T(8,128)}, u32[]{:S(2)}) copy-start(f32[6,128]{1,0:T(8,128)} %skip_ref.1) | copy-start | bytes 9220

commit v2 on v1

--- a/solution.py
+++ b/solution.py
@@ -23,8 +23,15 @@
     return jnp.maximum(x, 0.0) + jnp.where(u < 1e-3, u - 0.5 * u * u, jnp.log(1.0 + u))
 
 
-def column(tile, lane):
-    return jnp.broadcast_to(tile[:, lane : lane + 1], tile.shape)
+def dot_t(a, b):
+    return lax.dot_general(a, b, (((1,), (1,)), ((), ())), preferred_element_type=F32)
+
+
+def split_lanes(proj):
+    half = proj.shape[1] // 2
+    high = proj.astype(BF16).astype(F32)
+    lane = lax.broadcasted_iota(jnp.int32, proj.shape, 1)
+    return jnp.where(lane < half, high, pltpu.roll(proj - high, half, axis=1)).astype(BF16)
 
 
 def kernel(
@@ -45,8 +52,10 @@
     ow2,
     xwp,
     dtwp,
-    ratep,
     rates,
+    spread,
+    zspread,
+    lspread,
     nb,
     xs,
     yin,
@@ -59,13 +68,11 @@
     sgate,
     lstep,
     lu,
-    lproj,
     lout,
     zinner,
     comb,
     zstep,
     zu,
-    zproj,
     zskip,
     zout,
     zgate,
@@ -98,7 +105,7 @@
     mean_a = jnp.sum(jnp.where(low_half, squares, 0.0), axis=1, keepdims=True) * (1.0 / width)
     mean_b = jnp.sum(jnp.where(low_half, 0.0, squares), axis=1, keepdims=True) * (1.0 / width)
     scale = jnp.where(low_half, lax.rsqrt(mean_a + 1e-5), lax.rsqrt(mean_b + 1e-5))
-    normed = values * scale * gain_ref[...]
+    normed = values * scale * jnp.concatenate([gain_ref[...], gain_ref[...]], axis=1)
     nb[...] = normed.astype(BF16).reshape(nb.shape)
     for r in range(nrow):
         pieces = [
@@ -163,16 +170,17 @@
     w4[0:width, 2 * inner : 3 * inner] = inw_ref[:, inner : 2 * inner]
     w4[width : 2 * width, 3 * inner : 4 * inner] = inw_ref[:, inner : 2 * inner]
     ow2[...] = jnp.zeros_like(ow2)
-    ow2[0:inner, 0:width] = outw_ref[...]
-    ow2[inner : 2 * inner, width : 2 * width] = outw_ref[...]
+    ow2[0:width, 0:inner] = outw_ref[...]
+    ow2[width : 2 * width, inner : 2 * inner] = outw_ref[...]
     xwp[...] = jnp.zeros_like(xwp)
-    xwp[:, :, 0 : rank + 2 * state] = xw_ref[...]
+    xwp[:, 0 : rank + 2 * state, :] = xw_ref[...]
     dtwp[...] = jnp.zeros_like(dtwp)
     dtwp[:, 0:rank, :] = dtw_ref[...]
-    for d in range(6):
-        ratep[...] = jnp.zeros_like(ratep)
-        ratep[:, 0:state] = rate_ref[d] * (-LOG2E)
-        rates[d] = ratep[...].T[0:state]
+    rates[...] = rate_ref[...] * (-LOG2E)
+    source = lax.broadcasted_iota(jnp.int32, (inner, inner), 0)
+    for n in range(2 * state):
+        hit = (source == rank + n) | (source == inner // 2 + rank + n)
+        spread[:, n * inner : (n + 1) * inner] = jnp.where(hit, 1.0, 0.0).astype(BF16)
 
     rows = 2 * 2 * y_loc
     front = rows // 2
@@ -225,8 +233,8 @@
         row = lax.broadcasted_iota(jnp.int32, (chunk * rows, inner), 0)
         forward = lax.rem(row, rows) < front
         low = lax.rem(row, 2) == 0
-        p0 = jnp.dot(act_b, xwp[0], preferred_element_type=F32)
-        p1 = jnp.dot(act_b, xwp[1], preferred_element_type=F32)
+        p0 = dot_t(act_b, xwp[0])
+        p1 = dot_t(act_b, xwp[1])
         proj = jnp.where(forward, p0, p1)
         s0 = jnp.dot(proj, dtwp[0], precision=lax.Precision.HIGHEST, preferred_element_type=F32)
         s1 = jnp.dot(proj, dtwp[1], precision=lax.Precision.HIGHEST, preferred_element_type=F32)
@@ -235,7 +243,12 @@
         here = pl.ds(base, chunk * rows)
         zstep[here, :] = step
         zu[here, :] = step * act
-        zproj[here, :] = jnp.where(low, proj, pltpu.roll(proj, inner - state // 2, axis=1))
+        parts = split_lanes(jnp.where(low, proj, pltpu.roll(proj, inner - state // 2, axis=1)))
+        wide = state // 2 * inner
+        for g in range(2):
+            zspread[here, g * wide : (g + 1) * wide] = jnp.dot(
+                parts, spread[:, 2 * g * wide : (2 * g + 1) * wide], preferred_element_type=F32
+            )
         zskip[here, :] = (act.reshape(chunk, rows, inner) * zskipw[None]).reshape(
             chunk * rows, inner
         )
@@ -264,14 +277,19 @@
                 pre = pre + convw_ref[e, k : k + 1, :][None] * inn[first : first + length]
             act_b = silu(pre).reshape(total, inner).astype(BF16)
             act = act_b.astype(F32)
-            proj = jnp.dot(act_b, xwp[e], preferred_element_type=F32)
+            proj = dot_t(act_b, xwp[e])
             low = jnp.dot(
                 proj, dtwp[e], precision=lax.Precision.HIGHEST, preferred_element_type=F32
             )
             step = softplus(low + dtb_ref[e : e + 1, :])
             lstep[...] = step.reshape(lstep.shape)
             lu[...] = (step * act).reshape(lu.shape)
-            lproj[...] = proj.reshape(lproj.shape)
+            parts = split_lanes(proj)
+            for n in range(0, 2 * state, 4):
+                block = slice(n * inner, (n + 4) * inner)
+                lspread[:, :, block] = jnp.dot(
+                    parts, spread[:, block], preferred_element_type=F32
+                ).reshape(length, count, 4 * inner)
             skipped = (act * skip_ref[e : e + 1, :]).reshape(lout.shape)
             if direction == 0:
                 lout[...] = skipped
@@ -284,16 +302,17 @@
                 held = [jnp.zeros((8, inner), F32) for _ in range(state)]
                 for i in range(length):
                     t = i if direction == 0 else length - 1 - i
-                    step_t, u_t, proj_t = lstep[t, at, :], lu[t, at, :], lproj[t, at, :]
+                    step_t, u_t = lstep[t, at, :], lu[t, at, :]
                     result = lout[t, at, :]
                     for n in range(state):
-                        inflow = u_t * column(proj_t, rank + n)
+                        inflow = u_t * lspread[t, at, n * inner : (n + 1) * inner]
                         if i == 0:
                             held[n] = inflow
                         else:
                             decay = jnp.exp2(step_t * rates[e, n : n + 1, :])
                             held[n] = decay * held[n] + inflow
-                        result = result + held[n] * column(proj_t, rank + state + n)
+                        m = state + n
+                        result = result + held[n] * lspread[t, at, m * inner : (m + 1) * inner]
                     lout[t, at, :] = result
 
         hidden = [
@@ -302,7 +321,7 @@
             .astype(BF16)
             for par in range(2)
         ]
-        far = jnp.dot(jnp.concatenate(hidden, axis=1), ow2[...], preferred_element_type=F32)
+        far = dot_t(jnp.concatenate(hidden, axis=1), ow2[...])
         ret_ref[...] = far.astype(BF16).reshape(ret_ref.shape)
 
     for y in range(y_loc):
@@ -335,12 +354,13 @@
         for i in range(unroll):
             t = block * unroll + i
             at = pl.ds(pl.multiple_of(t * rows, rows), rows)
-            step_t, u_t, proj_t = zstep[at, :], zu[at, :], zproj[at, :]
+            step_t, u_t = zstep[at, :], zu[at, :]
             result = zskip[at, :]
             for n in range(halves):
                 decay = jnp.exp2(step_t * zrate[n])
-                held[n] = decay * held[n] + u_t * column(proj_t, rank + n)
-                result = result + held[n] * column(proj_t, rank + state + n)
+                held[n] = decay * held[n] + u_t * zspread[at, n * inner : (n + 1) * inner]
+                m = halves + n
+                result = result + held[n] * zspread[at, m * inner : (m + 1) * inner]
             zout[pl.ds(pl.multiple_of(t * rows, rows), front), :] = result[0:front]
             zout[pl.ds((z_cells - 1 - t) * rows + front, front), :] = result[front:]
         return tuple(held)
@@ -365,7 +385,7 @@
             pieces.append(total)
         along = jnp.concatenate(pieces, axis=0)
         near.append((along * zgate[:, par * inner : (par + 1) * inner]).astype(BF16))
-    acc[...] = jnp.dot(jnp.concatenate(near, axis=1), ow2[...], preferred_element_type=F32)
+    acc[...] = dot_t(jnp.concatenate(near, axis=1), ow2[...])
 
     yfar[my_col] = yret[pl.ds(my_col * y_loc, y_loc)]
     xfar[my_row] = xret[my_row]
@@ -414,7 +434,7 @@
         tokens = y_loc * half_z
         sizes = (nrow, ncol, y_loc, half_z, zpy, zpx, width, inner, state, rank)
         pairs = voxels.reshape(tokens, 2 * width)
-        gain = jnp.concatenate([norm_gain, norm_gain]).reshape(1, 2 * width)
+        gain = norm_gain.reshape(1, width)
         line = (nrow, 2 * zpy, inner)
         zrows = 4 * y_loc * z_cells
         taps = conv_weight.shape[1]
@@ -426,11 +446,13 @@
             out_specs=vmem,
             scratch_shapes=[
                 pltpu.VMEM((2 * width, 4 * inner), BF16),
-                pltpu.VMEM((2 * inner, 2 * width), BF16),
-                pltpu.VMEM((6, inner, 128), BF16),
+                pltpu.VMEM((2 * width, 2 * inner), BF16),
+                pltpu.VMEM((6, 128, inner), BF16),
                 pltpu.VMEM((6, 128, inner), F32),
-                pltpu.VMEM((inner, 128), F32),
                 pltpu.VMEM((6, state, inner), F32),
+                pltpu.VMEM((inner, 2 * state * inner), BF16),
+                pltpu.VMEM((zrows, state * inner), F32),
+                pltpu.VMEM((nrow, 2 * zpy, 2 * state * inner), F32),
                 pltpu.VMEM((y_loc, half_z, 2 * width), BF16),
                 pltpu.VMEM((nrow, y_loc * zpx, 2 * width), BF16),
                 pltpu.VMEM((y_full, zpy, 2 * width), BF16),
@@ -444,10 +466,8 @@
                 pltpu.VMEM(line, F32),
                 pltpu.VMEM(line, F32),
                 pltpu.VMEM(line, F32),
-                pltpu.VMEM(line, F32),
                 pltpu.VMEM((zrows, inner), F32),
                 pltpu.VMEM((zrows + (taps - 1) * 4 * y_loc, inner), F32),
-                pltpu.VMEM((zrows, inner), F32),
                 pltpu.VMEM((zrows, inner), F32),
                 pltpu.VMEM((zrows, inner), F32),
                 pltpu.VMEM((zrows, inner), F32),
@@ -464,7 +484,7 @@
                 pltpu.SemaphoreType.DMA((nrow,)),
             ],
             compiler_params=pltpu.CompilerParams(
-                collective_id=0, has_side_effects=True, vmem_limit_bytes=40 * 1024 * 1024
+                collective_id=0, has_side_effects=True, vmem_limit_bytes=52 * 1024 * 1024
             ),
         )(
             pairs,
@@ -472,12 +492,12 @@
             in_weight,
             conv_weight,
             conv_bias,
-            x_weight,
+            jnp.swapaxes(x_weight, 1, 2),
             dt_weight,
             dt_bias,
-            a_rate,
+            jnp.swapaxes(a_rate, 1, 2),
             skip_gain,
-            out_weight,
+            out_weight.T,
         )
         return out.reshape(voxels.shape)
 

time: 46.5 us -> 33.9 us (0.73)
  Pallas kernels: 41.4 us -> 29 us
  other arithmetic: 0.8 us -> 0 us
  local copies, waits for them, and re-layouts: 3.91 us -> 4.48 us
    pallas_call x1, Pallas kernels: 41.4 us -> 29 us  [local(): pl.pallas_call(functools.partial(kernel, sizes), out_shape=jax.ShapeDtype...]
    reshape x1 -> x0, other arithmetic: 0.8 us -> none  [local(): gain = jnp.concatenate([norm_gain, norm_gain]).reshape(1, 2 * width)]
    unnamed x19 -> x20, local copies, waits for them, and re-layouts: 2.36 us -> 2.87 us
where the time goes in v2:
time: 33.9 us; the launch traced here: 33.6 us
  Pallas kernels  29 us (86%)
  local copies, waits for them, and re-layouts  4.48 us (13%)
    pallas_call x1, Pallas kernels, local(): pl.pallas_call(functools.partial(kernel, sizes), out_shape=jax.ShapeDtype...  29 us
    unnamed x20, local copies, waits for them, and re-layouts  2.87 us
    reshape x1, local copies, waits for them, and re-layouts, local(): pairs = voxels.reshape(tokens, 2 * width)  0.95 us

profile of v2, /device:TPU:0, one launch (start us, length us, event | category | flops | bytes accessed | tf_op | source)
XLA Modules:
  0.0 33.6 jit_solution(2753323135391709852)
XLA Ops:
  0.0 0.0 copy-start.7
  0.0 0.0 copy-start.9
  0.0 0.0 copy-start
  0.0 0.0 copy-start.1
  0.0 0.0 copy-start.3
  0.0 0.0 copy-start.6
  0.0 1.0 %reshape.9.vox_ref = bf16[256,128]{1,0:T(8,128)(2,1)S(1)} reshape(bf16[1,2,16384]{2,1,0:T(2,128)(2,1)} %param.11) | data formatting | bytes 131072 | tf_op jit(solution)/shard_map/reshape | solution.py:436
  1.0 0.0 copy-done.7
  1.0 0.0 copy-done.9
  1.0 0.0 copy-done
  1.0 0.0 copy-done.1
  1.0 0.0 copy-done.3
  1.0 0.0 copy-done.6
  1.0 0.0 copy-start.2
  1.1 0.7 %copy-done.2 = bf16[64,256]{1,0:T(8,128)(2,1)S(1)} copy-done((bf16[64,256]{1,0:T(8,128)(2,1)S(1)}, bf16[64,256]{1,0:T(8,128)(2,1)}, u32[]{:S(2)}) %copy-start.2) | copy-done | bytes 32792
  1.8 0.0 copy-start.4
  1.8 0.7 %copy-done.4 = f32[6,4,128]{2,1,0:T(4,128)S(1)} copy-done((f32[6,4,128]{2,1,0:T(4,128)S(1)}, f32[6,4,128]{2,1,0:T(4,128)}, u32[]{:S(2)}) %copy-start.4) | copy-done | bytes 12312
  2.5 0.0 copy-start.5
  2.5 0.7 %copy-done.5 = f32[6,4,128]{2,1,0:T(4,128)S(1)} copy-done((f32[6,4,128]{2,1,0:T(4,128)S(1)}, f32[6,4,128]{2,1,0:T(4,128)}, u32[]{:S(2)}) %copy-start.5) | copy-done | bytes 12312
  3.2 0.0 copy-start.8
  3.2 0.7 %copy-done.8 = f32[6,128]{1,0:T(8,128)S(1)} copy-done((f32[6,128]{1,0:T(8,128)S(1)}, f32[6,128]{1,0:T(8,128)}, u32[]{:S(2)}) %copy-start.8) | copy-done | bytes 3096
  3.9 29.0 %shard_map.109 = bf16[256,128]{1,0:T(8,128)(2,1)S(1)} custom-call(bf16[256,128]{1,0:T(8,128)(2,1)S(1)} %reshape.9.vox_ref, f32[1,64]{1,0:T(1,128)S(1)} %bitcast.7, bf16[64,256]{1,0:T(8,128)(2,1)S(1)} %copy-done.2, f32[6,4,128]{2,1,0:T(4,128)S(1)} %copy-done.4, f32[6,128]{1,0:T(8,128)S(1)} %copy-done.6, bf16[6,36,128]{2,1,0:T(8,128)(2,1)S(1)} %bitcast.4, ...), custom_call_target="tpu_custom_call" | custom-call | tf_op jit(solution)/shard_map/pallas_call | solution.py:442
  32.9 0.7 %reshape.11 = bf16[1,2,16384]{2,1,0:T(2,128)(2,1)} reshape(bf16[256,128]{1,0:T(8,128)(2,1)S(1)} %shard_map.109) | data formatting | bytes 131072 | tf_op jit(solution)/shard_map/reshape | solution.py:502
Async XLA Ops:
  0.0 1.0 %copy-start.7 = (f32[6,128]{1,0:T(8,128)S(1)}, f32[6,128]{1,0:T(8,128)}, u32[]{:S(2)}) copy-start(f32[6,128]{1,0:T(8,128)} %dtb_ref.1) | copy-start | bytes 9220
  0.0 1.0 %copy-start.9 = (f32[64]{0:T(128)S(1)}, f32[64]{0:T(128)}, u32[]{:S(2)}) copy-start(f32[64]{0:T(128)} %param.12) | copy-start | bytes 772
  0.0 1.0 %copy-start = (bf16[6,128,36]{1,2,0:T(8,128)(2,1)S(1)}, bf16[6,128,36]{1,2,0:T(8,128)(2,1)}, u32[]{:S(2)}) copy-start(bf16[6,128,36]{1,2,0:T(8,128)(2,1)} %param.16) | copy-start | bytes 165892
  0.0 1.0 %copy-start.1 = (f32[6,128,16]{1,2,0:T(8,128)S(1)}, f32[6,128,16]{1,2,0:T(8,128)}, u32[]{:S(2)}) copy-start(f32[6,128,16]{1,2,0:T(8,128)} %param.19) | copy-start | bytes 147460
  0.0 1.0 %copy-start.3 = (bf16[128,64]{0,1:T(8,128)(2,1)S(1)}, bf16[128,64]{0,1:T(8,128)(2,1)}, u32[]{:S(2)}) copy-start(bf16[128,64]{0,1:T(8,128)(2,1)} %param.21) | copy-start | bytes 49156
  0.0 1.0 %copy-start.6 = (f32[6,128]{1,0:T(8,128)S(1)}, f32[6,128]{1,0:T(8,128)}, u32[]{:S(2)}) copy-start(f32[6,128]{1,0:T(8,128)} %convb_ref.1) | copy-start | bytes 9220
  1.0 0.8 %copy-start.2 = (bf16[64,256]{1,0:T(8,128)(2,1)S(1)}, bf16[64,256]{1,0:T(8,128)(2,1)}, u32[]{:S(2)}) copy-start(bf16[64,256]{1,0:T(8,128)(2,1)} %inw_ref.1) | copy-start | bytes 98308
  1.8 0.7 %copy-start.4 = (f32[6,4,128]{2,1,0:T(4,128)S(1)}, f32[6,4,128]{2,1,0:T(4,128)}, u32[]{:S(2)}) copy-start(f32[6,4,128]{2,1,0:T(4,128)} %convw_ref.1) | copy-start | bytes 36868
  2.5 0.7 %copy-start.5 = (f32[6,4,128]{2,1,0:T(4,128)S(1)}, f32[6,4,128]{2,1,0:T(4,128)}, u32[]{:S(2)}) copy-start(f32[6,4,128]{2,1,0:T(4,128)} %dtw_ref.1) | copy-start | bytes 36868
  3.2 0.7 %copy-start.8 = (f32[6,128]{1,0:T(8,128)S(1)}, f32[6,128]{1,0:T(8,128)}, u32[]{:S(2)}) copy-start(f32[6,128]{1,0:T(8,128)} %skip_ref.1) | copy-start | bytes 9220

commit v3 on v2

--- a/solution.py
+++ b/solution.py
@@ -38,6 +38,16 @@
     sizes,
     vox_ref,
     gain_ref,
+    inw_hbm,
+    convw_hbm,
+    convb_hbm,
+    xw_hbm,
+    dtw_hbm,
+    dtb_hbm,
+    rate_hbm,
+    skip_hbm,
+    outw_hbm,
+    out_ref,
     inw_ref,
     convw_ref,
     convb_ref,
@@ -47,7 +57,7 @@
     rate_ref,
     skip_ref,
     outw_ref,
-    out_ref,
+    wsem,
     w4,
     ow2,
     xwp,
@@ -90,6 +100,22 @@
     my_row, my_col = lax.axis_index("row"), lax.axis_index("col")
     z_cells = 2 * half_z
 
+    weights = (
+        (inw_hbm, inw_ref),
+        (convw_hbm, convw_ref),
+        (convb_hbm, convb_ref),
+        (xw_hbm, xw_ref),
+        (dtw_hbm, dtw_ref),
+        (dtb_hbm, dtb_ref),
+        (rate_hbm, rate_ref),
+        (skip_hbm, skip_ref),
+        (outw_hbm, outw_ref),
+    )
+    fetches = [
+        pltpu.make_async_copy(far, near, wsem.at[i]) for i, (far, near) in enumerate(weights)
+    ]
+    for fetch in fetches:
+        fetch.start()
     barrier = pltpu.get_barrier_semaphore()
     for k in range(1, ncol):
         peer = lax.rem(my_col + k, ncol)
@@ -164,6 +190,8 @@
     for k in range(1, nrow):
         x_go(k).start()
 
+    for fetch in fetches:
+        fetch.wait()
     w4[...] = jnp.zeros_like(w4)
     w4[0:width, 0:inner] = inw_ref[:, 0:inner]
     w4[width : 2 * width, inner : 2 * inner] = inw_ref[:, 0:inner]
@@ -439,12 +467,25 @@
         zrows = 4 * y_loc * z_cells
         taps = conv_weight.shape[1]
         vmem = pl.BlockSpec(memory_space=pltpu.VMEM)
+        weights = (
+            in_weight,
+            conv_weight,
+            conv_bias,
+            jnp.swapaxes(x_weight, 1, 2),
+            dt_weight,
+            dt_bias,
+            jnp.swapaxes(a_rate, 1, 2),
+            skip_gain,
+            out_weight.T,
+        )
         out = pl.pallas_call(
             functools.partial(kernel, sizes),
             out_shape=jax.ShapeDtypeStruct((tokens, 2 * width), BF16),
-            in_specs=[vmem] * 11,
+            in_specs=[vmem] * 2 + [pl.BlockSpec(memory_space=pltpu.HBM)] * 9,
             out_specs=vmem,
             scratch_shapes=[
+                *[pltpu.VMEM(w.shape, w.dtype) for w in weights],
+                pltpu.SemaphoreType.DMA((len(weights),)),
                 pltpu.VMEM((2 * width, 4 * inner), BF16),
                 pltpu.VMEM((2 * width, 2 * inner), BF16),
                 pltpu.VMEM((6, 128, inner), BF16),
@@ -484,20 +525,12 @@
                 pltpu.SemaphoreType.DMA((nrow,)),
             ],
             compiler_params=pltpu.CompilerParams(
-                collective_id=0, has_side_effects=True, vmem_limit_bytes=52 * 1024 * 1024
+                collective_id=0, has_side_effects=True, vmem_limit_bytes=64 * 1024 * 1024
             ),
         )(
             pairs,
             gain,
-            in_weight,
-            conv_weight,
-            conv_bias,
-            jnp.swapaxes(x_weight, 1, 2),
-            dt_weight,
-            dt_bias,
-            jnp.swapaxes(a_rate, 1, 2),
-            skip_gain,
-            out_weight.T,
+            *weights,
         )
         return out.reshape(voxels.shape)
 

time: 33.9 us -> 33.8 us (level)
  Pallas kernels: 29 us -> 30.5 us
  local copies, waits for them, and re-layouts: 4.48 us -> 3.02 us
    unnamed x20 -> x0, local copies, waits for them, and re-layouts: 2.87 us -> none
    pallas_call x1, Pallas kernels: 29 us -> 30.5 us  [local(): pl.pallas_call(functools.partial(kernel, sizes), out_shape=jax.ShapeDtype...]
    reshape x1, local copies, waits for them, and re-layouts: 0.65 us -> 1.49 us  [local(): return out.reshape(voxels.shape)]
    reshape x1, local copies, waits for them, and re-layouts: 0.95 us -> 1.53 us  [local(): pairs = voxels.reshape(tokens, 2 * width)]
where the time goes in v3:
time: 33.8 us; the launch traced here: 33.5 us
  Pallas kernels  30.5 us (90%)
  local copies, waits for them, and re-layouts  3.02 us (9%)
    pallas_call x1, Pallas kernels, local(): pl.pallas_call(functools.partial(kernel, sizes), out_shape=jax.ShapeDtype...  30.5 us
    reshape x1, local copies, waits for them, and re-layouts, local(): pairs = voxels.reshape(tokens, 2 * width)  1.53 us
    reshape x1, local copies, waits for them, and re-layouts, local(): return out.reshape(voxels.shape)  1.49 us

profile of v3, /device:TPU:0, one launch (start us, length us, event | category | flops | bytes accessed | tf_op | source)
XLA Modules:
  0.0 33.5 jit_solution(7822704508835121536)
XLA Ops:
  0.0 1.5 %reshape.9.vox_ref = bf16[256,128]{1,0:T(8,128)(2,1)} reshape(bf16[1,2,16384]{2,1,0:T(2,128)(2,1)} %param.11) | data formatting | bytes 131072 | tf_op jit(solution)/shard_map/reshape | solution.py:464
  1.5 30.5 %shard_map.109 = bf16[256,128]{1,0:T(8,128)(2,1)} custom-call(bf16[256,128]{1,0:T(8,128)(2,1)} %reshape.9.vox_ref, f32[1,64]{1,0:T(1,128)} %bitcast.7, bf16[64,256]{1,0:T(8,128)(2,1)} %inw_hbm.1, f32[6,4,128]{2,1,0:T(4,128)} %convw_hbm.1, f32[6,128]{1,0:T(8,128)} %convb_hbm.1, bf16[6,36,128]{2,1,0:T(8,128)(2,1)} %bitcast.4, f32[6,4,128]{2,1,0:T(4,128)} %dtw_hbm.1, ...), custom_call_target="tpu_custom_call" | custom-call | tf_op jit(solution)/shard_map/pallas_call | solution.py:481
  32.0 1.5 %reshape.11 = bf16[1,2,16384]{2,1,0:T(2,128)(2,1)} reshape(bf16[256,128]{1,0:T(8,128)(2,1)} %shard_map.109) | data formatting | bytes 131072 | tf_op jit(solution)/shard_map/reshape | solution.py:535

commit v4 on v3

--- a/solution.py
+++ b/solution.py
@@ -65,7 +65,11 @@
     rates,
     spread,
     zspread,
-    lspread,
+    w2t,
+    owd,
+    cols,
+    lrows,
+    lhid,
     nb,
     xs,
     yin,
@@ -74,11 +78,12 @@
     xret,
     yfar,
     xfar,
-    inn,
-    sgate,
+    linn,
+    lgate,
     lstep,
     lu,
     lout,
+    lproj,
     zinner,
     comb,
     zstep,
@@ -205,6 +210,30 @@
     dtwp[...] = jnp.zeros_like(dtwp)
     dtwp[:, 0:rank, :] = dtw_ref[...]
     rates[...] = rate_ref[...] * (-LOG2E)
+    w2 = jnp.concatenate([inw_ref[...], inw_ref[...]], axis=0).astype(F32)
+    w2t[0:inner, :] = w2[:, 0:inner].T.astype(BF16)
+    w2t[inner : 2 * inner, :] = w2[:, inner : 2 * inner].T.astype(BF16)
+    owd[0:width, :] = outw_ref[...]
+    owd[width : 2 * width, :] = outw_ref[...]
+    taps = convw_ref.shape[1]
+    proj_rows = 48
+    count = cols.shape[3]
+    line = lax.broadcasted_iota(jnp.int32, (128, inner), 0)
+    for axis in range(2):
+        d = 2 * axis + 2
+
+        def put(at, up, down):
+            cols[axis, at] = jnp.where(line < count // 2, up, down).T[:, 0:count]
+
+        for k in range(taps):
+            put(k, convw_ref[d, k : k + 1, :], convw_ref[d + 1, k : k + 1, :])
+        put(taps, convb_ref[d : d + 1, :], convb_ref[d + 1 : d + 2, :])
+        put(taps + 1, dtb_ref[d : d + 1, :], dtb_ref[d + 1 : d + 2, :])
+        put(taps + 2, skip_ref[d : d + 1, :], skip_ref[d + 1 : d + 2, :])
+        for r in range(rank):
+            put(taps + 3 + r, dtw_ref[d, r : r + 1, :], dtw_ref[d + 1, r : r + 1, :])
+        for n in range(state):
+            put(taps + 3 + rank + n, rates[d, n : n + 1, :], rates[d + 1, n : n + 1, :])
     source = lax.broadcasted_iota(jnp.int32, (inner, inner), 0)
     for n in range(2 * state):
         hit = (source == rank + n) | (source == inner // 2 + rank + n)
@@ -226,7 +255,6 @@
                 for low in range(2):
                     start = par * rows + direction * front + y * 2 + low
                     zinner[pl.ds(start, half_z, stride=2 * rows), :] = piece
-    taps = convw_ref.shape[1]
     pad = taps - 1
     comb[0 : pad * rows, :] = jnp.zeros((pad * rows, inner), F32)
 
@@ -283,74 +311,71 @@
 
     def lines(src_ref, ret_ref, d):
         length, pairs = src_ref.shape[0], src_ref.shape[1]
-        count = 2 * pairs
-        total = length * count
-        both = jnp.dot(
-            src_ref[...].reshape(length * pairs, 2 * width), w4[...], preferred_element_type=F32
-        )
-        inn[0:pad] = jnp.zeros((pad, count, inner), F32)
-        inn[pad + length :] = jnp.zeros((pad, count, inner), F32)
-        for par in range(2):
-            part = both[:, par * inner : (par + 1) * inner].astype(BF16).astype(F32)
-            inn[pad : pad + length, par * pairs : (par + 1) * pairs, :] = part.reshape(
-                length, pairs, inner
-            )
-            gate = both[:, (2 + par) * inner : (3 + par) * inner]
-            sgate[:, par * pairs : (par + 1) * pairs, :] = silu(gate).reshape(length, pairs, inner)
-        for direction in range(2):
-            e = d + direction
-            pre = convb_ref[e : e + 1, :][None]
+        count = 4 * pairs
+        half = count // 2
+        lane = lax.broadcasted_iota(jnp.int32, (length, pairs, 2 * width), 2)
+        raw = src_ref[...].astype(F32)
+        lower = jnp.where(lane < width, raw, 0.0).astype(BF16)
+        upper = jnp.where(lane < width, 0.0, raw).astype(BF16)
+        for t in range(length):
+            back = length - 1 - t
+            lrows[t, 0:pairs] = lower[t]
+            lrows[t, pairs:half] = upper[t]
+            lrows[t, half : half + pairs] = lower[back]
+            lrows[t, half + pairs :] = upper[back]
+        linn[0:pad] = jnp.zeros((pad, inner, count), F32)
+        for t in range(length):
+            both = dot_t(w2t[...], lrows[t])
+            linn[pad + t] = both[0:inner].astype(BF16).astype(F32)
+            lgate[t] = silu(both[inner:])
+        upward = lax.broadcasted_iota(jnp.int32, (proj_rows, count), 1) < half
+        for t in range(length):
+            pre = cols[d // 2 - 1, taps]
             for k in range(taps):
-                first = k if direction == 0 else 2 * pad - k
-                pre = pre + convw_ref[e, k : k + 1, :][None] * inn[first : first + length]
-            act_b = silu(pre).reshape(total, inner).astype(BF16)
+                pre = pre + cols[d // 2 - 1, k] * linn[t + k]
+            act_b = silu(pre).astype(BF16)
             act = act_b.astype(F32)
-            proj = dot_t(act_b, xwp[e])
-            low = jnp.dot(
-                proj, dtwp[e], precision=lax.Precision.HIGHEST, preferred_element_type=F32
-            )
-            step = softplus(low + dtb_ref[e : e + 1, :])
-            lstep[...] = step.reshape(lstep.shape)
-            lu[...] = (step * act).reshape(lu.shape)
-            parts = split_lanes(proj)
-            for n in range(0, 2 * state, 4):
-                block = slice(n * inner, (n + 4) * inner)
-                lspread[:, :, block] = jnp.dot(
-                    parts, spread[:, block], preferred_element_type=F32
-                ).reshape(length, count, 4 * inner)
-            skipped = (act * skip_ref[e : e + 1, :]).reshape(lout.shape)
-            if direction == 0:
-                lout[...] = skipped
-            else:
-                lout[...] += skipped
-
-            @pl.loop(0, count // 8)
-            def _(group):
-                at = pl.ds(pl.multiple_of(group * 8, 8), 8)
-                held = [jnp.zeros((8, inner), F32) for _ in range(state)]
-                for i in range(length):
-                    t = i if direction == 0 else length - 1 - i
-                    step_t, u_t = lstep[t, at, :], lu[t, at, :]
-                    result = lout[t, at, :]
-                    for n in range(state):
-                        inflow = u_t * lspread[t, at, n * inner : (n + 1) * inner]
-                        if i == 0:
-                            held[n] = inflow
+            p0 = jnp.dot(xwp[d, 0:proj_rows], act_b, preferred_element_type=F32)
+            p1 = jnp.dot(xwp[d + 1, 0:proj_rows], act_b, preferred_element_type=F32)
+            proj = jnp.where(upward, p0, p1)
+            lproj[t] = proj
+            low = cols[d // 2 - 1, taps + 1]
+            for r in range(rank):
+                low = low + cols[d // 2 - 1, taps + 3 + r] * proj[r : r + 1, :]
+            step = softplus(low)
+            lstep[t] = step
+            lu[t] = step * act
+            lout[t] = cols[d // 2 - 1, taps + 2] * act
+
+        depth, block = 16, state // 2
+
+        @pl.loop(0, inner // depth)
+        def _(tile):
+            at = pl.ds(pl.multiple_of(tile * depth, depth), depth)
+            for first in range(0, state, block):
+                held = [None] * block
+                for t in range(length):
+                    step_t, u_t, result = lstep[t, at, :], lu[t, at, :], lout[t, at, :]
+                    for m in range(block):
+                        n = first + m
+                        inflow = u_t * lproj[t, rank + n : rank + n + 1, :]
+                        if t == 0:
+                            held[m] = inflow
                         else:
-                            decay = jnp.exp2(step_t * rates[e, n : n + 1, :])
-                            held[n] = decay * held[n] + inflow
-                        m = state + n
-                        result = result + held[n] * lspread[t, at, m * inner : (m + 1) * inner]
+                            rate = cols[d // 2 - 1, taps + 3 + rank + n, at, :]
+                            held[m] = jnp.exp2(step_t * rate) * held[m] + inflow
+                        c = rank + state + n
+                        result = result + held[m] * lproj[t, c : c + 1, :]
                     lout[t, at, :] = result
 
-        hidden = [
-            (lout[:, par * pairs : (par + 1) * pairs, :] * sgate[:, par * pairs : (par + 1) * pairs, :])
-            .reshape(length * pairs, inner)
-            .astype(BF16)
-            for par in range(2)
-        ]
-        far = dot_t(jnp.concatenate(hidden, axis=1), ow2[...])
-        ret_ref[...] = far.astype(BF16).reshape(ret_ref.shape)
+        for t in range(length):
+            lhid[t] = (lout[t] * lgate[t]).T.astype(BF16)
+        share = dot_t(lhid[...].reshape(length * count, inner), owd[...])
+        first_half = lax.broadcasted_iota(jnp.int32, (pairs, 2 * width), 1) < width
+        for t in range(length):
+            start, back = t * count, (length - 1 - t) * count + half
+            both = share[start : start + half] + share[back : back + half]
+            ret_ref[t] = jnp.where(first_half, both[0:pairs], both[pairs:]).astype(BF16)
 
     for y in range(y_loc):
         yin[my_col * y_loc + y] = nb[y, pl.ds(pl.multiple_of(my_col * zpy, zpy), zpy), :]
@@ -463,7 +488,8 @@
         sizes = (nrow, ncol, y_loc, half_z, zpy, zpx, width, inner, state, rank)
         pairs = voxels.reshape(tokens, 2 * width)
         gain = norm_gain.reshape(1, width)
-        line = (nrow, 2 * zpy, inner)
+        count = 4 * zpy
+        line = (nrow, inner, count)
         zrows = 4 * y_loc * z_cells
         taps = conv_weight.shape[1]
         vmem = pl.BlockSpec(memory_space=pltpu.VMEM)
@@ -493,7 +519,11 @@
                 pltpu.VMEM((6, state, inner), F32),
                 pltpu.VMEM((inner, 2 * state * inner), BF16),
                 pltpu.VMEM((zrows, state * inner), F32),
-                pltpu.VMEM((nrow, 2 * zpy, 2 * state * inner), F32),
+                pltpu.VMEM((2 * inner, 2 * width), BF16),
+                pltpu.VMEM((2 * width, inner), BF16),
+                pltpu.VMEM((2, taps + 3 + rank + state, inner, count), F32),
+                pltpu.VMEM((nrow, count, 2 * width), BF16),
+                pltpu.VMEM((nrow, count, inner), BF16),
                 pltpu.VMEM((y_loc, half_z, 2 * width), BF16),
                 pltpu.VMEM((nrow, y_loc * zpx, 2 * width), BF16),
                 pltpu.VMEM((y_full, zpy, 2 * width), BF16),
@@ -502,11 +532,12 @@
                 pltpu.VMEM((nrow, y_loc * zpx, 2 * width), BF16),
                 pltpu.VMEM((ncol, y_loc, zpy, 2 * width), BF16),
                 pltpu.VMEM((nrow, y_loc * zpx, 2 * width), BF16),
-                pltpu.VMEM((nrow + 2 * (taps - 1), 2 * zpy, inner), F32),
+                pltpu.VMEM((nrow + taps - 1, inner, count), F32),
                 pltpu.VMEM(line, F32),
                 pltpu.VMEM(line, F32),
                 pltpu.VMEM(line, F32),
                 pltpu.VMEM(line, F32),
+                pltpu.VMEM((nrow, 48, count), F32),
                 pltpu.VMEM((zrows, inner), F32),
                 pltpu.VMEM((zrows + (taps - 1) * 4 * y_loc, inner), F32),
                 pltpu.VMEM((zrows, inner), F32),

time: 33.8 us -> 29.5 us (0.87)
  Pallas kernels: 30.5 us -> 26.2 us
    pallas_call x1, Pallas kernels: 30.5 us -> 26.2 us  [local(): pl.pallas_call(functools.partial(kernel, sizes), out_shape=jax.ShapeDtype...]
where the time goes in v4:
time: 29.5 us; the launch traced here: 29.2 us
  Pallas kernels  26.2 us (89%)
  local copies, waits for them, and re-layouts  3.02 us (10%)
    pallas_call x1, Pallas kernels, local(): pl.pallas_call(functools.partial(kernel, sizes), out_shape=jax.ShapeDtype...  26.2 us
    reshape x1, local copies, waits for them, and re-layouts, local(): pairs = voxels.reshape(tokens, 2 * width)  1.53 us
    reshape x1, local copies, waits for them, and re-layouts, local(): return out.reshape(voxels.shape)  1.49 us

profile of v4, /device:TPU:0, one launch (start us, length us, event | category | flops | bytes accessed | tf_op | source)
XLA Modules:
  0.0 29.2 jit_solution(17980659118869143184)
XLA Ops:
  0.0 1.5 %reshape.9.vox_ref = bf16[256,128]{1,0:T(8,128)(2,1)} reshape(bf16[1,2,16384]{2,1,0:T(2,128)(2,1)} %param.11) | data formatting | bytes 131072 | tf_op jit(solution)/shard_map/reshape | solution.py:489
  1.5 26.2 %shard_map.109 = bf16[256,128]{1,0:T(8,128)(2,1)} custom-call(bf16[256,128]{1,0:T(8,128)(2,1)} %reshape.9.vox_ref, f32[1,64]{1,0:T(1,128)} %bitcast.7, bf16[64,256]{1,0:T(8,128)(2,1)} %inw_hbm.1, f32[6,4,128]{2,1,0:T(4,128)} %convw_hbm.1, f32[6,128]{1,0:T(8,128)} %convb_hbm.1, bf16[6,36,128]{2,1,0:T(8,128)(2,1)} %bitcast.4, f32[6,4,128]{2,1,0:T(4,128)} %dtw_hbm.1, ...), custom_call_target="tpu_custom_call" | custom-call | tf_op jit(solution)/shard_map/pallas_call | solution.py:507
  27.8 1.5 %reshape.11 = bf16[1,2,16384]{2,1,0:T(2,128)(2,1)} reshape(bf16[256,128]{1,0:T(8,128)(2,1)} %shard_map.109) | data formatting | bytes 131072 | tf_op jit(solution)/shard_map/reshape | solution.py:566

commit v5 on v4

--- a/solution.py
+++ b/solution.py
@@ -31,7 +31,7 @@
     half = proj.shape[1] // 2
     high = proj.astype(BF16).astype(F32)
     lane = lax.broadcasted_iota(jnp.int32, proj.shape, 1)
-    return jnp.where(lane < half, high, pltpu.roll(proj - high, half, axis=1)).astype(BF16)
+    return jnp.where(lane < half, high, pltpu.roll(proj - high, half, axis=1))
 
 
 def kernel(
@@ -64,7 +64,9 @@
     dtwp,
     rates,
     spread,
-    zspread,
+    zparts,
+    spread_a,
+    spread_b,
     w2t,
     owd,
     cols,
@@ -129,7 +131,14 @@
         peer = lax.rem(my_row + k, nrow)
         pl.semaphore_signal(barrier, inc=1, device_id=(peer, my_col), device_id_type=MESH)
 
-    values = vox_ref[...].astype(F32)
+    @pl.loop(0, half_z // 8)
+    def _(block):
+        for i in range(8):
+            pair = block * 8 + i
+            there = pl.ds(pl.multiple_of(pair * 2 * width, 2 * width), 2 * width)
+            acc[pl.ds(pair, y_loc, stride=half_z), :] = vox_ref[:, there].astype(F32)
+
+    values = acc[...]
     squares = values * values
     lane = lax.broadcasted_iota(jnp.int32, values.shape, 1)
     low_half = lane < width
@@ -208,7 +217,13 @@
     xwp[...] = jnp.zeros_like(xwp)
     xwp[:, 0 : rank + 2 * state, :] = xw_ref[...]
     dtwp[...] = jnp.zeros_like(dtwp)
-    dtwp[:, 0:rank, :] = dtw_ref[...]
+    for d in range(2):
+        whole = dtw_ref[d]
+        high = whole.astype(BF16)
+        rest = (whole - high.astype(F32)).astype(BF16)
+        for base in (0, inner // 2):
+            dtwp[base : base + rank, d * inner : (d + 1) * inner] = high
+            dtwp[base : base + rank, (2 + d) * inner : (3 + d) * inner] = rest
     rates[...] = rate_ref[...] * (-LOG2E)
     w2 = jnp.concatenate([inw_ref[...], inw_ref[...]], axis=0).astype(F32)
     w2t[0:inner, :] = w2[:, 0:inner].T.astype(BF16)
@@ -292,19 +307,18 @@
         p0 = dot_t(act_b, xwp[0])
         p1 = dot_t(act_b, xwp[1])
         proj = jnp.where(forward, p0, p1)
-        s0 = jnp.dot(proj, dtwp[0], precision=lax.Precision.HIGHEST, preferred_element_type=F32)
-        s1 = jnp.dot(proj, dtwp[1], precision=lax.Precision.HIGHEST, preferred_element_type=F32)
+        parts = split_lanes(proj)
+        lowered = jnp.dot(parts.astype(BF16), dtwp[...], preferred_element_type=F32)
+        s0 = lowered[:, 0:inner] + lowered[:, 2 * inner : 3 * inner]
+        s1 = lowered[:, inner : 2 * inner] + lowered[:, 3 * inner : 4 * inner]
         step = jnp.where(forward, s0, s1).reshape(chunk, rows, inner) + zdtb[None]
         step = softplus(step).reshape(chunk * rows, inner)
         here = pl.ds(base, chunk * rows)
         zstep[here, :] = step
         zu[here, :] = step * act
-        parts = split_lanes(jnp.where(low, proj, pltpu.roll(proj, inner - state // 2, axis=1)))
-        wide = state // 2 * inner
-        for g in range(2):
-            zspread[here, g * wide : (g + 1) * wide] = jnp.dot(
-                parts, spread[:, 2 * g * wide : (2 * g + 1) * wide], preferred_element_type=F32
-            )
+        zparts[here, :] = jnp.where(
+            low, parts, pltpu.roll(parts, inner - state // 2, axis=1)
+        ).astype(BF16)
         zskip[here, :] = (act.reshape(chunk, rows, inner) * zskipw[None]).reshape(
             chunk * rows, inner
         )
@@ -400,27 +414,47 @@
         )
         for n in range(halves)
     ]
-    unroll = 8
-
-    def advance(block, held):
-        held = list(held)
-        for i in range(unroll):
-            t = block * unroll + i
+    wide = halves * inner
+    blocks = z_cells // chunk
+
+    def widen(block, target):
+        here = pl.ds(pl.multiple_of(block * (chunk * rows), chunk * rows), chunk * rows)
+        for g in range(2):
+            target[:, g * wide : (g + 1) * wide] = jnp.dot(
+                zparts[here, :],
+                spread[:, 2 * g * wide : (2 * g + 1) * wide],
+                preferred_element_type=F32,
+            )
+
+    def scan_block(block, source, held):
+        for i in range(chunk):
+            t = block * chunk + i
             at = pl.ds(pl.multiple_of(t * rows, rows), rows)
             step_t, u_t = zstep[at, :], zu[at, :]
+            own = slice(i * rows, (i + 1) * rows)
             result = zskip[at, :]
             for n in range(halves):
                 decay = jnp.exp2(step_t * zrate[n])
-                held[n] = decay * held[n] + u_t * zspread[at, n * inner : (n + 1) * inner]
+                held[n] = decay * held[n] + u_t * source[own, n * inner : (n + 1) * inner]
                 m = halves + n
-                result = result + held[n] * zspread[at, m * inner : (m + 1) * inner]
+                result = result + held[n] * source[own, m * inner : (m + 1) * inner]
             zout[pl.ds(pl.multiple_of(t * rows, rows), front), :] = result[0:front]
             zout[pl.ds((z_cells - 1 - t) * rows + front, front), :] = result[front:]
+        return held
+
+    widen(0, spread_a)
+
+    def advance(pair, held):
+        held = list(held)
+        widen(2 * pair + 1, spread_b)
+        held = scan_block(2 * pair, spread_a, held)
+        widen(lax.rem(2 * pair + 2, blocks), spread_a)
+        held = scan_block(2 * pair + 1, spread_b, held)
         return tuple(held)
 
     lax.fori_loop(
         0,
-        z_cells // unroll,
+        blocks // 2,
         advance,
         tuple(jnp.zeros((rows, inner), F32) for _ in range(halves)),
     )
@@ -455,7 +489,13 @@
             acc[y * half_z + r * zpx : y * half_z + (r + 1) * zpx, :] += part[
                 y * zpx : (y + 1) * zpx
             ]
-    out_ref[...] = acc[...].astype(BF16)
+
+    @pl.loop(0, half_z // 8)
+    def _(block):
+        for i in range(8):
+            pair = block * 8 + i
+            there = pl.ds(pl.multiple_of(pair * 2 * width, 2 * width), 2 * width)
+            out_ref[:, there] = acc[pl.ds(pair, y_loc, stride=half_z), :].astype(BF16)
 
 
 def solution(mesh):
@@ -486,7 +526,7 @@
         assert y_full == nrow and zpy == y_loc * zpx
         tokens = y_loc * half_z
         sizes = (nrow, ncol, y_loc, half_z, zpy, zpx, width, inner, state, rank)
-        pairs = voxels.reshape(tokens, 2 * width)
+        pairs = voxels.reshape(y_loc, merged)
         gain = norm_gain.reshape(1, width)
         count = 4 * zpy
         line = (nrow, inner, count)
@@ -506,7 +546,7 @@
         )
         out = pl.pallas_call(
             functools.partial(kernel, sizes),
-            out_shape=jax.ShapeDtypeStruct((tokens, 2 * width), BF16),
+            out_shape=jax.ShapeDtypeStruct((y_loc, merged), BF16),
             in_specs=[vmem] * 2 + [pl.BlockSpec(memory_space=pltpu.HBM)] * 9,
             out_specs=vmem,
             scratch_shapes=[
@@ -515,10 +555,12 @@
                 pltpu.VMEM((2 * width, 4 * inner), BF16),
                 pltpu.VMEM((2 * width, 2 * inner), BF16),
                 pltpu.VMEM((6, 128, inner), BF16),
-                pltpu.VMEM((6, 128, inner), F32),
+                pltpu.VMEM((inner, 4 * inner), BF16),
                 pltpu.VMEM((6, state, inner), F32),
                 pltpu.VMEM((inner, 2 * state * inner), BF16),
-                pltpu.VMEM((zrows, state * inner), F32),
+                pltpu.VMEM((zrows, inner), BF16),
+                pltpu.VMEM((32 * 4 * y_loc, state * inner), F32),
+                pltpu.VMEM((32 * 4 * y_loc, state * inner), F32),
                 pltpu.VMEM((2 * inner, 2 * width), BF16),
                 pltpu.VMEM((2 * width, inner), BF16),
                 pltpu.VMEM((2, taps + 3 + rank + state, inner, count), F32),

time: 29.5 us -> 25.8 us (0.87)
  Pallas kernels: 26.2 us -> 24.1 us
  local copies, waits for them, and re-layouts: 3.02 us -> 1.52 us
    reshape x2 -> x0, local copies, waits for them, and re-layouts: 3.02 us -> none  [the longest x1 1.53 us: local(): pairs = voxels.reshape(tokens, 2 * width)]
    pallas_call x1, Pallas kernels: 26.2 us -> 24.1 us  [local(): pl.pallas_call(functools.partial(kernel, sizes), out_shape=jax.ShapeDtype...]
    unnamed x0 -> x1, local copies, waits for them, and re-layouts: none -> 1.52 us
where the time goes in v5:
time: 25.8 us; the launch traced here: 25.6 us
  Pallas kernels  24.1 us (93%)
  local copies, waits for them, and re-layouts  1.52 us (6%)
    pallas_call x1, Pallas kernels, local(): pl.pallas_call(functools.partial(kernel, sizes), out_shape=jax.ShapeDtype...  24.1 us
    unnamed x1, local copies, waits for them, and re-layouts  1.52 us

profile of v5, /device:TPU:0, one launch (start us, length us, event | category | flops | bytes accessed | tf_op | source)
XLA Modules:
  0.0 25.6 jit_solution(15238342986819536528)
XLA Ops:
  0.0 24.1 %shard_map.109 = bf16[2,16384]{1,0:T(2,128)(2,1)} custom-call(bf16[2,16384]{1,0:T(2,128)(2,1)} %bitcast.7, f32[1,64]{1,0:T(1,128)} %bitcast.11, bf16[64,256]{1,0:T(8,128)(2,1)} %inw_hbm.1, f32[6,4,128]{2,1,0:T(4,128)} %convw_hbm.1, f32[6,128]{1,0:T(8,128)} %convb_hbm.1, bf16[6,36,128]{2,1,0:T(8,128)(2,1)} %bitcast.8, f32[6,4,128]{2,1,0:T(4,128)} %dtw_hbm.1, ...), custom_call_target="tpu_custom_call" | custom-call | tf_op jit(solution)/shard_map/pallas_call | solution.py:547
  24.1 1.5 %copy.13 = bf16[1,2,16384]{2,1,0:T(2,128)(2,1)} copy(bf16[1,2,16384]{2,1,0:T(2,128)(2,1)} %bitcast.6) | data formatting | bytes 131072

commit v6 on v5

--- a/solution.py
+++ b/solution.py
@@ -36,8 +36,8 @@
 
 def kernel(
     sizes,
-    vox_ref,
-    gain_ref,
+    vox_hbm,
+    gain_hbm,
     inw_hbm,
     convw_hbm,
     convb_hbm,
@@ -48,6 +48,8 @@
     skip_hbm,
     outw_hbm,
     out_ref,
+    vox_ref,
+    gain_ref,
     inw_ref,
     convw_ref,
     convb_ref,
@@ -108,6 +110,8 @@
     z_cells = 2 * half_z
 
     weights = (
+        (vox_hbm, vox_ref),
+        (gain_hbm, gain_ref),
         (inw_hbm, inw_ref),
         (convw_hbm, convw_ref),
         (convb_hbm, convb_ref),
@@ -131,6 +135,9 @@
         peer = lax.rem(my_row + k, nrow)
         pl.semaphore_signal(barrier, inc=1, device_id=(peer, my_col), device_id_type=MESH)
 
+    for fetch in fetches[:2]:
+        fetch.wait()
+
     @pl.loop(0, half_z // 8)
     def _(block):
         for i in range(8):
@@ -204,7 +211,7 @@
     for k in range(1, nrow):
         x_go(k).start()
 
-    for fetch in fetches:
+    for fetch in fetches[2:]:
         fetch.wait()
     w4[...] = jnp.zeros_like(w4)
     w4[0:width, 0:inner] = inw_ref[:, 0:inner]
@@ -292,35 +299,36 @@
     zskipw = jnp.where(lowhalf8, by_dir(skip_ref[0:1, :], skip_ref[1:2, :]), 0.0)
     chunk = 32
 
-    @pl.loop(0, z_cells // chunk)
+    large = z_cells // 2
+
+    @pl.loop(0, z_cells // large)
     def _(block):
-        base = pl.multiple_of(block * (chunk * rows), chunk * rows)
+        base = pl.multiple_of(block * (large * rows), large * rows)
         pre = zbias[None]
         for k in range(taps):
-            tap = comb[pl.ds(base + k * rows, chunk * rows), :]
-            pre = pre + zconv[k][None] * tap.reshape(chunk, rows, inner)
-        act_b = silu(pre).reshape(chunk * rows, inner).astype(BF16)
+            tap = comb[pl.ds(base + k * rows, large * rows), :]
+            pre = pre + zconv[k][None] * tap.reshape(large, rows, inner)
+        act_b = silu(pre).reshape(large * rows, inner).astype(BF16)
         act = act_b.astype(F32)
-        row = lax.broadcasted_iota(jnp.int32, (chunk * rows, inner), 0)
+        row = lax.broadcasted_iota(jnp.int32, (large * rows, inner), 0)
         forward = lax.rem(row, rows) < front
         low = lax.rem(row, 2) == 0
-        p0 = dot_t(act_b, xwp[0])
-        p1 = dot_t(act_b, xwp[1])
-        proj = jnp.where(forward, p0, p1)
+        either = dot_t(act_b, xwp[0:2].reshape(2 * inner, inner))
+        proj = jnp.where(forward, either[:, 0:inner], either[:, inner:])
         parts = split_lanes(proj)
         lowered = jnp.dot(parts.astype(BF16), dtwp[...], preferred_element_type=F32)
         s0 = lowered[:, 0:inner] + lowered[:, 2 * inner : 3 * inner]
         s1 = lowered[:, inner : 2 * inner] + lowered[:, 3 * inner : 4 * inner]
-        step = jnp.where(forward, s0, s1).reshape(chunk, rows, inner) + zdtb[None]
-        step = softplus(step).reshape(chunk * rows, inner)
-        here = pl.ds(base, chunk * rows)
+        step = jnp.where(forward, s0, s1).reshape(large, rows, inner) + zdtb[None]
+        step = softplus(step).reshape(large * rows, inner)
+        here = pl.ds(base, large * rows)
         zstep[here, :] = step
         zu[here, :] = step * act
         zparts[here, :] = jnp.where(
             low, parts, pltpu.roll(parts, inner - state // 2, axis=1)
         ).astype(BF16)
-        zskip[here, :] = (act.reshape(chunk, rows, inner) * zskipw[None]).reshape(
-            chunk * rows, inner
+        zskip[here, :] = (act.reshape(large, rows, inner) * zskipw[None]).reshape(
+            large * rows, inner
         )
 
     def lines(src_ref, ret_ref, d):
@@ -342,6 +350,7 @@
             both = dot_t(w2t[...], lrows[t])
             linn[pad + t] = both[0:inner].astype(BF16).astype(F32)
             lgate[t] = silu(both[inner:])
+        x_maps = jnp.concatenate([xwp[d, 0:proj_rows], xwp[d + 1, 0:proj_rows]], axis=0)
         upward = lax.broadcasted_iota(jnp.int32, (proj_rows, count), 1) < half
         for t in range(length):
             pre = cols[d // 2 - 1, taps]
@@ -349,9 +358,8 @@
                 pre = pre + cols[d // 2 - 1, k] * linn[t + k]
             act_b = silu(pre).astype(BF16)
             act = act_b.astype(F32)
-            p0 = jnp.dot(xwp[d, 0:proj_rows], act_b, preferred_element_type=F32)
-            p1 = jnp.dot(xwp[d + 1, 0:proj_rows], act_b, preferred_element_type=F32)
-            proj = jnp.where(upward, p0, p1)
+            either = jnp.dot(x_maps, act_b, preferred_element_type=F32)
+            proj = jnp.where(upward, either[0:proj_rows], either[proj_rows:])
             lproj[t] = proj
             low = cols[d // 2 - 1, taps + 1]
             for r in range(rank):
@@ -533,7 +541,9 @@
         zrows = 4 * y_loc * z_cells
         taps = conv_weight.shape[1]
         vmem = pl.BlockSpec(memory_space=pltpu.VMEM)
-        weights = (
+        operands = (
+            pairs,
+            gain,
             in_weight,
             conv_weight,
             conv_bias,
@@ -547,11 +557,11 @@
         out = pl.pallas_call(
             functools.partial(kernel, sizes),
             out_shape=jax.ShapeDtypeStruct((y_loc, merged), BF16),
-            in_specs=[vmem] * 2 + [pl.BlockSpec(memory_space=pltpu.HBM)] * 9,
+            in_specs=[pl.BlockSpec(memory_space=pltpu.HBM)] * len(operands),
             out_specs=vmem,
             scratch_shapes=[
-                *[pltpu.VMEM(w.shape, w.dtype) for w in weights],
-                pltpu.SemaphoreType.DMA((len(weights),)),
+                *[pltpu.VMEM(w.shape, w.dtype) for w in operands],
+                pltpu.SemaphoreType.DMA((len(operands),)),
                 pltpu.VMEM((2 * width, 4 * inner), BF16),
                 pltpu.VMEM((2 * width, 2 * inner), BF16),
                 pltpu.VMEM((6, 128, inner), BF16),
@@ -601,9 +611,7 @@
                 collective_id=0, has_side_effects=True, vmem_limit_bytes=64 * 1024 * 1024
             ),
         )(
-            pairs,
-            gain,
-            *weights,
+            *operands,
         )
         return out.reshape(voxels.shape)
 

time: 25.8 us -> 23.2 us (0.90)
  Pallas kernels: 24.1 us -> 21.4 us
    pallas_call x1, Pallas kernels: 24.1 us -> 21.4 us  [local(): pl.pallas_call(functools.partial(kernel, sizes), out_shape=jax.ShapeDtype...]
where the time goes in v6:
time: 23.2 us; the launch traced here: 23 us
  Pallas kernels  21.4 us (92%)
  local copies, waits for them, and re-layouts  1.52 us (7%)
    pallas_call x1, Pallas kernels, local(): pl.pallas_call(functools.partial(kernel, sizes), out_shape=jax.ShapeDtype...  21.4 us
    unnamed x1, local copies, waits for them, and re-layouts  1.52 us

profile of v6, /device:TPU:0, one launch (start us, length us, event | category | flops | bytes accessed | tf_op | source)
XLA Modules:
  0.0 23.0 jit_solution(15470325248053905457)
XLA Ops:
  0.0 21.4 %shard_map.109 = bf16[2,16384]{1,0:T(2,128)(2,1)} custom-call(bf16[2,16384]{1,0:T(2,128)(2,1)} %bitcast.7, f32[1,64]{1,0:T(1,128)} %bitcast.11, bf16[64,256]{1,0:T(8,128)(2,1)} %inw_hbm.1, f32[6,4,128]{2,1,0:T(4,128)} %convw_hbm.1, f32[6,128]{1,0:T(8,128)} %convb_hbm.1, bf16[6,36,128]{2,1,0:T(8,128)(2,1)} %bitcast.8, f32[6,4,128]{2,1,0:T(4,128)} %dtw_hbm.1, ...), custom_call_target="tpu_custom_call" | custom-call | tf_op jit(solution)/shard_map/pallas_call | solution.py:557
  21.4 1.5 %copy.13 = bf16[1,2,16384]{2,1,0:T(2,128)(2,1)} copy(bf16[1,2,16384]{2,1,0:T(2,128)(2,1)} %bitcast.6) | data formatting | bytes 131072
